TPU v7x, 512 devices: a whole 4x8x8 slice. The times are simulated.
512 devices in a mesh: ctx: 32 (over y, x), mp: 16 (over z, core).
Axes of the slice: x: 4, y: 8, z: 8, core: 2. Of those that a mesh axis runs over, the one named last changes fastest.
Arguments:
- gate_in: bfloat16 [4096, 8192], P('ctx', 'mp'), may hold values from -6 to 6
- value_in: bfloat16 [4096, 8192], P('ctx', 'mp'), may hold values from -6 to 6
- gate_out: bfloat16 [4096, 8192], P('ctx', 'mp'), may hold values from -7 to 7
- filter_taps: float32 [4096, 8192], P('ctx', 'mp'), may hold values from -1 to 1
- skip_gain: float32 [8192], P('mp'), may hold values from 0.1 to 1.9
- queries: bfloat16 [4096, 8192], P('ctx', 'mp'), may hold values from -8 to 8
- key_rows: bfloat16 [4096, 8192], P('ctx', 'mp'), may hold values from -8 to 8
Outputs:
- mixer_out: bfloat16 [4096, 8192], P('ctx', 'mp')
- attended: bfloat16 [4096, 8192], P('ctx', 'mp')
All inputs are finite; a program needn't handle non-finite values.
Results may differ from a plain program's by a relative error of at most 0.0059.
Values may be sent and summed in bfloat16 or wider, within the bound.
A program may use at most 64 MiB of HBM per device.

v0:
```python
import math

import jax
import jax.numpy as jnp
from jax import lax
from jax.sharding import PartitionSpec as P

D = 8192
HEAD_DIM = 128
SPAN = 4


def swapped(value, axis, stride):
    mask = 2**stride
    pairs = [(source, source ^ mask) for source in range(lax.axis_size(axis))]
    return lax.ppermute(value, axis, pairs)


def shifted(block, axis, distance):
    devices = range(lax.axis_size(axis))
    route = [(i - distance, i) for i in devices if i - distance in devices]
    return lax.ppermute(block, axis, route)


def complex_product(a_real, a_imag, b_real, b_imag):
    return (a_real * b_real - a_imag * b_imag, a_real * b_imag + a_imag * b_real)


def phase_table(first, second, extent, direction):
    phase_turns = first * second % extent
    angles = phase_turns.astype(jnp.float32) * (direction * 2.0 * math.pi / extent)
    return (jnp.cos(angles), jnp.sin(angles))


def local_transform(real_part, imag_part, direction):
    extent = real_part.shape[1]
    indices = jnp.arange(extent, dtype=jnp.int32)
    cos_table, sin_table = phase_table(indices[:, None], indices[None, :], extent, direction)

    def contract(matrix, operand):
        return jnp.einsum("br,src->sbc", matrix, operand, precision=lax.Precision.HIGHEST)

    return (
        contract(cos_table, real_part) - contract(sin_table, imag_part),
        contract(cos_table, imag_part) + contract(sin_table, real_part),
    )


def butterfly_forward(real_part, imag_part):
    device_index = lax.axis_index("ctx")
    section_count = lax.axis_size("ctx").bit_length() - 1
    for section_idx in range(section_count):
        bit_index = section_count - 1 - section_idx
        half_span = 1 << bit_index
        if section_idx == 0:
            partner_real, partner_tail = swapped((real_part, imag_part[2:]), "ctx", bit_index)
            partner_imag = jnp.concatenate([jnp.zeros_like(partner_tail), partner_tail], 0)
        else:
            partner_real, partner_imag = swapped((real_part, imag_part), "ctx", bit_index)
        upper_half = device_index >> bit_index & 1 == 1
        low_bits = device_index & half_span - 1
        angles = low_bits.astype(jnp.float32) * (-math.pi / half_span)
        diff_real, diff_imag = complex_product(
            partner_real - real_part, partner_imag - imag_part, jnp.cos(angles), jnp.sin(angles)
        )
        real_part = jnp.where(upper_half, diff_real, real_part + partner_real)
        imag_part = jnp.where(upper_half, diff_imag, imag_part + partner_imag)
    return (real_part, imag_part)


def butterfly_inverse(real_part, imag_part):
    device_index = lax.axis_index("ctx")
    section_count = lax.axis_size("ctx").bit_length() - 1
    for bit_index in range(section_count):
        half_span = 1 << bit_index
        partner_real, partner_imag = swapped((real_part, imag_part), "ctx", bit_index)
        upper_half = device_index >> bit_index & 1 == 1
        low_bits = device_index & half_span - 1
        angles = low_bits.astype(jnp.float32) * (math.pi / half_span)
        twist_real, twist_imag = (jnp.cos(angles), jnp.sin(angles))
        mine_real, mine_imag = complex_product(real_part, imag_part, twist_real, twist_imag)
        their_real, their_imag = complex_product(partner_real, partner_imag, twist_real, twist_imag)
        real_part, imag_part = (
            jnp.where(upper_half, partner_real - mine_real, real_part + their_real),
            jnp.where(upper_half, partner_imag - mine_imag, imag_part + their_imag),
        )
    return (real_part, imag_part)


def reversed_place(device_index, section_count):
    result = jnp.zeros((), jnp.int32)
    for bit_index in range(section_count):
        result = result + (device_index >> bit_index & 1) * (1 << section_count - 1 - bit_index)
    return result


def panel_convolution(signal, filter_taps, position, length):
    device_index = lax.axis_index("ctx")
    row_count = signal.shape[0]
    section_count = lax.axis_size("ctx").bit_length() - 1
    half_angles = position.astype(jnp.float32)[:, None] * (-math.pi / length)
    half_real, half_imag = (jnp.cos(half_angles), jnp.sin(half_angles))
    zero_field = jnp.zeros_like(signal)
    real_part = jnp.stack([signal, filter_taps, signal * half_real, filter_taps * half_real])
    imag_part = jnp.stack([zero_field, zero_field, signal * half_imag, filter_taps * half_imag])
    row_index = jnp.arange(row_count, dtype=jnp.int32)[:, None]
    real_part, imag_part = butterfly_forward(real_part, imag_part)
    frequency = reversed_place(device_index, section_count)
    twist_real, twist_imag = phase_table(row_index, frequency, length, -1)
    real_part, imag_part = complex_product(real_part, imag_part, twist_real, twist_imag)
    real_part, imag_part = local_transform(real_part, imag_part, -1)
    prod_real, prod_imag = complex_product(
        real_part[0::2], imag_part[0::2], real_part[1::2], imag_part[1::2]
    )
    real_part, imag_part = local_transform(prod_real, prod_imag, 1)
    frequency = reversed_place(device_index, section_count)
    twist_real, twist_imag = phase_table(row_index, frequency, length, 1)
    real_part, imag_part = complex_product(real_part, imag_part, twist_real, twist_imag)
    real_part, imag_part = butterfly_inverse(real_part, imag_part)
    return (real_part[0] + half_real * real_part[1] + half_imag * imag_part[1]) * (0.5 / length)


def local(gate_in, value_in, gate_out, filter_taps, skip_gain, queries, key_rows):
    device_index = lax.axis_index("ctx")
    ctx_count = lax.axis_size("ctx")
    row_count = gate_in.shape[0]
    length = row_count * ctx_count
    signal = gate_in.astype(jnp.float32) * value_in.astype(jnp.float32)
    position = device_index * row_count + jnp.arange(row_count, dtype=jnp.int32)
    convolved = panel_convolution(signal, filter_taps, position, length)
    mixer_full = gate_out.astype(jnp.float32) * (convolved + skip_gain[None, :] * signal)
    mixer_out = mixer_full.astype(jnp.bfloat16)
    widened = mixer_out.astype(jnp.float32)
    row_power = lax.psum(jnp.sum(widened * widened, axis=1), "mp")
    row_scale = lax.rsqrt(row_power / D + 1e-06)
    values = (widened * row_scale[:, None]).astype(jnp.bfloat16)
    window_parts = [(key_rows, values)]
    carried = (key_rows, values)
    for distance in range(SPAN):
        carried = shifted((carried[0], carried[1]), "ctx", 1)
        window_parts.append(carried)
    window_keys = jnp.concatenate([entry_pair[0] for entry_pair in reversed(window_parts)], 0)
    window_values = jnp.concatenate([entry_pair[1] for entry_pair in reversed(window_parts)], 0)
    local_heads = queries.shape[1] // HEAD_DIM
    query_heads = queries.reshape(row_count, local_heads, HEAD_DIM)
    key_heads = window_keys.reshape(-1, local_heads, HEAD_DIM)
    value_heads = window_values.reshape(-1, local_heads, HEAD_DIM)
    scores = jnp.einsum("qhd,khd->hqk", query_heads, key_heads, preferred_element_type=jnp.float32)
    scores = scores * (1.0 / math.sqrt(HEAD_DIM))
    key_position = (device_index - SPAN) * row_count + jnp.arange(
        (SPAN + 1) * row_count, dtype=jnp.int32
    )
    allowed = (
        (key_position[None, :] <= position[:, None])
        & (key_position[None, :] > position[:, None] - SPAN * row_count)
        & (key_position[None, :] >= 0)
    )
    scores = jnp.where(allowed[None], scores, -1e30)
    row_top = jnp.max(scores, axis=2, keepdims=True)
    weights = jnp.exp(scores - row_top)
    denominator = jnp.sum(weights, axis=2, keepdims=True)
    rounded_weights = weights.astype(jnp.bfloat16)
    summed = jnp.einsum(
        "hqk,khd->qhd", rounded_weights, value_heads, preferred_element_type=jnp.float32
    )
    attended = summed / jnp.transpose(denominator, (1, 0, 2))
    return (mixer_out, attended.reshape(row_count, -1).astype(jnp.bfloat16))


def solution(mesh):
    return jax.shard_map(
        local,
        mesh=mesh,
        in_specs=(
            P("ctx", "mp"),
            P("ctx", "mp"),
            P("ctx", "mp"),
            P("ctx", "mp"),
            P("mp"),
            P("ctx", "mp"),
            P("ctx", "mp"),
        ),
        out_specs=(P("ctx", "mp"), P("ctx", "mp")),
        check_vma=False,
    )
```

profile of v0, /device:TPU:16, one launch (start us, length us, event | category | flops | bytes accessed | tf_op | source)
XLA Modules:
  0.0 608.0 jit_solution(916724548252071522)
XLA Ops:
  5.0 5.9 collective-permute-start
  15.7 65.5 %collective-permute-done.1 = f32[2,128,512]{1,2,0:T(8,128)S(1)} collective-permute-done((f32[2,128,512]{1,2,0:T(8,128)}, f32[2,128,512]{1,2,0:T(8,128)S(1)}, u32[]{:S(2)}, u32[]{:S(2)}) %collective-permute-start.1) | collective-permute-done | bytes 524320 | tf_op jit(solution)/shard_map/ppermute | solution.py:16
  91.9 61.0 %collective-permute-done.3 = f32[4,128,512]{1,2,0:T(8,128)} collective-permute-done((f32[4,128,512]{1,2,0:T(8,128)S(1)}, f32[4,128,512]{1,2,0:T(8,128)}, u32[]{:S(2)}, u32[]{:S(2)}) %collective-permute-start.3) | collective-permute-done | bytes 1048608 | tf_op jit(solution)/shard_map/ppermute | solution.py:16
  152.9 22.5 %collective-permute-done.2 = f32[4,128,512]{1,2,0:T(8,128)} collective-permute-done((f32[4,128,512]{1,2,0:T(8,128)}, f32[4,128,512]{1,2,0:T(8,128)}, u32[]{:S(2)}, u32[]{:S(2)}) %collective-permute-start.2) | collective-permute-done | bytes 1048608 | tf_op jit(solution)/shard_map/ppermute | solution.py:16
  184.7 21.9 %collective-permute-done.4 = f32[4,128,512]{1,2,0:T(8,128)S(1)} collective-permute-done((f32[4,128,512]{1,2,0:T(8,128)S(1)}, f32[4,128,512]{1,2,0:T(8,128)S(1)}, u32[]{:S(2)}, u32[]{:S(2)}) %collective-permute-start.4) | collective-permute-done | bytes 1048608 | tf_op jit(solution)/shard_map/ppermute | solution.py:16
  207.6 20.7 %collective-permute-done.5 = f32[4,128,512]{1,2,0:T(8,128)} collective-permute-done((f32[4,128,512]{1,2,0:T(8,128)}, f32[4,128,512]{1,2,0:T(8,128)}, u32[]{:S(2)}, u32[]{:S(2)}) %collective-permute-start.5) | collective-permute-done | bytes 1048608 | tf_op jit(solution)/shard_map/ppermute | solution.py:16
  238.1 22.0 %collective-permute-done.6 = f32[4,128,512]{1,2,0:T(8,128)S(1)} collective-permute-done((f32[4,128,512]{1,2,0:T(8,128)S(1)}, f32[4,128,512]{1,2,0:T(8,128)S(1)}, u32[]{:S(2)}, u32[]{:S(2)}) %collective-permute-start.6) | collective-permute-done | bytes 1048608 | tf_op jit(solution)/shard_map/ppermute | solution.py:16
  261.0 19.7 %collective-permute-done.7 = f32[4,128,512]{1,2,0:T(8,128)} collective-permute-done((f32[4,128,512]{1,2,0:T(8,128)S(1)}, f32[4,128,512]{1,2,0:T(8,128)}, u32[]{:S(2)}, u32[]{:S(2)}) %collective-permute-start.7) | collective-permute-done | bytes 1048608 | tf_op jit(solution)/shard_map/ppermute | solution.py:16
  289.3 21.8 %collective-permute-done.8 = f32[4,128,512]{1,2,0:T(8,128)S(1)} collective-permute-done((f32[4,128,512]{1,2,0:T(8,128)S(1)}, f32[4,128,512]{1,2,0:T(8,128)S(1)}, u32[]{:S(2)}, u32[]{:S(2)}) %collective-permute-start.8) | collective-permute-done | bytes 1048608 | tf_op jit(solution)/shard_map/ppermute | solution.py:16
  311.1 19.8 %collective-permute-done.9 = f32[4,128,512]{1,2,0:T(8,128)} collective-permute-done((f32[4,128,512]{1,2,0:T(8,128)S(1)}, f32[4,128,512]{1,2,0:T(8,128)}, u32[]{:S(2)}, u32[]{:S(2)}) %collective-permute-start.9) | collective-permute-done | bytes 1048608 | tf_op jit(solution)/shard_map/ppermute | solution.py:16
  346.8 10.9 %collective-permute-done.10 = f32[2,128,512]{1,2,0:T(8,128)S(1)} collective-permute-done((f32[2,128,512]{1,2,0:T(8,128)S(1)}, f32[2,128,512]{1,2,0:T(8,128)S(1)}, u32[]{:S(2)}, u32[]{:S(2)}) %collective-permute-start.10) | collective-permute-done | bytes 524320 | tf_op jit(solution)/shard_map/ppermute | solution.py:16
  357.6 7.5 %collective-permute-done.11 = f32[2,128,512]{1,2,0:T(8,128)S(1)} collective-permute-done((f32[2,128,512]{1,2,0:T(8,128)S(1)}, f32[2,128,512]{1,2,0:T(8,128)S(1)}, u32[]{:S(2)}, u32[]{:S(2)}) %collective-permute-start.11) | collective-permute-done | bytes 524320 | tf_op jit(solution)/shard_map/ppermute | solution.py:16
  373.0 10.7 %collective-permute-done.12 = f32[2,128,512]{1,2,0:T(8,128)S(1)} collective-permute-done((f32[2,128,512]{1,2,0:T(8,128)S(1)}, f32[2,128,512]{1,2,0:T(8,128)S(1)}, u32[]{:S(2)}, u32[]{:S(2)}) %collective-permute-start.12) | collective-permute-done | bytes 524320 | tf_op jit(solution)/shard_map/ppermute | solution.py:16
  383.7 6.6 %collective-permute-done.13 = f32[2,128,512]{1,2,0:T(8,128)S(1)} collective-permute-done((f32[2,128,512]{1,2,0:T(8,128)S(1)}, f32[2,128,512]{1,2,0:T(8,128)S(1)}, u32[]{:S(2)}, u32[]{:S(2)}) %collective-permute-start.13) | collective-permute-done | bytes 524320 | tf_op jit(solution)/shard_map/ppermute | solution.py:16
  396.7 10.7 %collective-permute-done.14 = f32[2,128,512]{1,2,0:T(8,128)S(1)} collective-permute-done((f32[2,128,512]{1,2,0:T(8,128)S(1)}, f32[2,128,512]{1,2,0:T(8,128)S(1)}, u32[]{:S(2)}, u32[]{:S(2)}) %collective-permute-start.14) | collective-permute-done | bytes 524320 | tf_op jit(solution)/shard_map/ppermute | solution.py:16
  407.4 5.8 collective-permute-done.15
  425.5 40.4 %collective-permute-done.24 = bf16[128,512]{0,1:T(8,128)(2,1)S(1)} collective-permute-done((bf16[128,512]{0,1:T(8,128)(2,1)S(1)}, bf16[128,512]{0,1:T(8,128)(2,1)S(1)}, u32[]{:S(2)}, u32[]{:S(2)}) %collective-permute-start.24) | collective-permute-done | bytes 131104 | tf_op jit(solution)/shard_map/ppermute | solution.py:22
  467.9 44.0 %collective-permute-done.25 = bf16[128,512]{0,1:T(8,128)(2,1)} collective-permute-done((bf16[128,512]{0,1:T(8,128)(2,1)S(1)}, bf16[128,512]{0,1:T(8,128)(2,1)}, u32[]{:S(2)}, u32[]{:S(2)}) %collective-permute-start.25) | collective-permute-done | bytes 131104 | tf_op jit(solution)/shard_map/ppermute | solution.py:22
  528.4 6.4 %collective-permute-done.27 = bf16[128,512]{0,1:T(8,128)(2,1)S(1)} collective-permute-done((bf16[128,512]{0,1:T(8,128)(2,1)}, bf16[128,512]{0,1:T(8,128)(2,1)S(1)}, u32[]{:S(2)}, u32[]{:S(2)}) %collective-permute-start.27) | collective-permute-done | bytes 131104 | tf_op jit(solution)/shard_map/ppermute | solution.py:22
  540.3 29.7 %psum.7 = f32[128]{0:T(128)S(1)} all-reduce(f32[128]{0:T(128)S(1)} %get-tuple-element.6), channel_id=1, replica_groups=mesh['ctx'=32,'mp'=16] {'mp'}, use_global_device_ids=true, to_apply=%region_1.2 | all-reduce | flops 128 | bytes 1024 | tf_op jit(solution)/shard_map/psum | solution.py:134
  573.9 5.9 collective-permute-done.20
  582.7 6.1 collective-permute-done.21
  591.1 6.6 %collective-permute-done.22 = bf16[128,512]{0,1:T(8,128)(2,1)S(1)} collective-permute-done((bf16[128,512]{0,1:T(8,128)(2,1)S(1)}, bf16[128,512]{0,1:T(8,128)(2,1)S(1)}, u32[]{:S(2)}, u32[]{:S(2)}) %collective-permute-start.22) | collective-permute-done | bytes 131104 | tf_op jit(solution)/shard_map/ppermute | solution.py:22
  600.6 6.1 collective-permute-done.23
  (109 shorter events, 127.3 us)
Async XLA Ops:
  5.0 76.2 %collective-permute-start = (f32[4,128,512]{1,2,0:T(8,128)}, f32[4,128,512]{1,2,0:T(8,128)S(1)}, u32[]{:S(2)}, u32[]{:S(2)}) collective-permute-start(f32[4,128,512]{1,2,0:T(8,128)} %pad_maximum_fusion), channel_id=1, source_target_pairs={{0,256},{16,272},{32,288},{48,304},{64,320},{80,336},{96,352},{112... | collective-permute-start | bytes 3145736 | tf_op jit(solution)/shard_map/ppermute | solution.py:16
  11.8 69.4 %collective-permute-start.1 = (f32[2,128,512]{1,2,0:T(8,128)}, f32[2,128,512]{1,2,0:T(8,128)S(1)}, u32[]{:S(2)}, u32[]{:S(2)}) collective-permute-start(f32[2,128,512]{1,2,0:T(8,128)} %pad_maximum_fusion.2), channel_id=1, source_target_pairs={{0,256},{16,272},{32,288},{48,304},{64,320},{80,336},{96,352},{112... | collective-permute-start | bytes 1572872 | tf_op jit(solution)/shard_map/ppermute | solution.py:16
  83.8 69.1 %collective-permute-start.3 = (f32[4,128,512]{1,2,0:T(8,128)S(1)}, f32[4,128,512]{1,2,0:T(8,128)}, u32[]{:S(2)}, u32[]{:S(2)}) collective-permute-start(f32[4,128,512]{1,2,0:T(8,128)S(1)} %fusion.8), channel_id=1, source_target_pairs={{0,128},{16,144},{32,160},{48,176},{64,192},{80,208},{96,224},{112... | collective-permute-start | bytes 3145736 | tf_op jit(solution)/shard_map/ppermute | solution.py:16
  87.0 88.5 %collective-permute-start.2 = (f32[4,128,512]{1,2,0:T(8,128)}, f32[4,128,512]{1,2,0:T(8,128)}, u32[]{:S(2)}, u32[]{:S(2)}) collective-permute-start(f32[4,128,512]{1,2,0:T(8,128)} %add_select_fusion.8), channel_id=1, source_target_pairs={{0,128},{16,144},{32,160},{48,176},{64,192},{80,208},{96,224},{112... | collective-permute-start | bytes 3145736 | tf_op jit(solution)/shard_map/ppermute | solution.py:16
  178.7 27.9 %collective-permute-start.4 = (f32[4,128,512]{1,2,0:T(8,128)S(1)}, f32[4,128,512]{1,2,0:T(8,128)S(1)}, u32[]{:S(2)}, u32[]{:S(2)}) collective-permute-start(f32[4,128,512]{1,2,0:T(8,128)S(1)} %get-tuple-element.14), channel_id=1, source_target_pairs={{0,64},{16,80},{32,96},{48,112},{64,0},{80,16},{96,32},{112,48},{1... | collective-permute-start | bytes 3145736 | tf_op jit(solution)/shard_map/ppermute | solution.py:16
  181.9 46.3 %collective-permute-start.5 = (f32[4,128,512]{1,2,0:T(8,128)}, f32[4,128,512]{1,2,0:T(8,128)}, u32[]{:S(2)}, u32[]{:S(2)}) collective-permute-start(f32[4,128,512]{1,2,0:T(8,128)} %get-tuple-element.15), channel_id=1, source_target_pairs={{0,64},{16,80},{32,96},{48,112},{64,0},{80,16},{96,32},{112,48},{1... | collective-permute-start | bytes 3145736 | tf_op jit(solution)/shard_map/ppermute | solution.py:16
  230.6 29.5 %collective-permute-start.6 = (f32[4,128,512]{1,2,0:T(8,128)S(1)}, f32[4,128,512]{1,2,0:T(8,128)S(1)}, u32[]{:S(2)}, u32[]{:S(2)}) collective-permute-start(f32[4,128,512]{1,2,0:T(8,128)S(1)} %get-tuple-element.12), channel_id=1, source_target_pairs={{0,32},{16,48},{32,0},{48,16},{64,96},{80,112},{96,64},{112,80},{1... | collective-permute-start | bytes 3145736 | tf_op jit(solution)/shard_map/ppermute | solution.py:16
  235.5 45.3 %collective-permute-start.7 = (f32[4,128,512]{1,2,0:T(8,128)S(1)}, f32[4,128,512]{1,2,0:T(8,128)}, u32[]{:S(2)}, u32[]{:S(2)}) collective-permute-start(f32[4,128,512]{1,2,0:T(8,128)S(1)} %get-tuple-element.13), channel_id=1, source_target_pairs={{0,32},{16,48},{32,0},{48,16},{64,96},{80,112},{96,64},{112,80},{1... | collective-permute-start | bytes 3145736 | tf_op jit(solution)/shard_map/ppermute | solution.py:16
  283.1 28.0 %collective-permute-start.8 = (f32[4,128,512]{1,2,0:T(8,128)S(1)}, f32[4,128,512]{1,2,0:T(8,128)S(1)}, u32[]{:S(2)}, u32[]{:S(2)}) collective-permute-start(f32[4,128,512]{1,2,0:T(8,128)S(1)} %get-tuple-element.10), channel_id=1, source_target_pairs={{0,16},{16,0},{32,48},{48,32},{64,80},{80,64},{96,112},{112,96},{1... | collective-permute-start | bytes 3145736 | tf_op jit(solution)/shard_map/ppermute | solution.py:16
  286.5 44.4 %collective-permute-start.9 = (f32[4,128,512]{1,2,0:T(8,128)S(1)}, f32[4,128,512]{1,2,0:T(8,128)}, u32[]{:S(2)}, u32[]{:S(2)}) collective-permute-start(f32[4,128,512]{1,2,0:T(8,128)S(1)} %get-tuple-element.11), channel_id=1, source_target_pairs={{0,16},{16,0},{32,48},{48,32},{64,80},{80,64},{96,112},{112,96},{1... | collective-permute-start | bytes 3145736 | tf_op jit(solution)/shard_map/ppermute | solution.py:16
  340.9 16.8 %collective-permute-start.10 = (f32[2,128,512]{1,2,0:T(8,128)S(1)}, f32[2,128,512]{1,2,0:T(8,128)S(1)}, u32[]{:S(2)}, u32[]{:S(2)}) collective-permute-start(f32[2,128,512]{1,2,0:T(8,128)S(1)} %get-tuple-element.27), channel_id=1, source_target_pairs={{0,16},{16,0},{32,48},{48,32},{64,80},{80,64},{96,112},{112,96},{1... | collective-permute-start | bytes 1572872 | tf_op jit(solution)/shard_map/ppermute | solution.py:16
  344.3 20.9 %collective-permute-start.11 = (f32[2,128,512]{1,2,0:T(8,128)S(1)}, f32[2,128,512]{1,2,0:T(8,128)S(1)}, u32[]{:S(2)}, u32[]{:S(2)}) collective-permute-start(f32[2,128,512]{1,2,0:T(8,128)S(1)} %get-tuple-element.26), channel_id=1, source_target_pairs={{0,16},{16,0},{32,48},{48,32},{64,80},{80,64},{96,112},{112,96},{1... | collective-permute-start | bytes 1572872 | tf_op jit(solution)/shard_map/ppermute | solution.py:16
  365.4 18.3 %collective-permute-start.12 = (f32[2,128,512]{1,2,0:T(8,128)S(1)}, f32[2,128,512]{1,2,0:T(8,128)S(1)}, u32[]{:S(2)}, u32[]{:S(2)}) collective-permute-start(f32[2,128,512]{1,2,0:T(8,128)S(1)} %get-tuple-element.23), channel_id=1, source_target_pairs={{0,32},{16,48},{32,0},{48,16},{64,96},{80,112},{96,64},{112,80},{1... | collective-permute-start | bytes 1572872 | tf_op jit(solution)/shard_map/ppermute | solution.py:16
  370.4 19.9 %collective-permute-start.13 = (f32[2,128,512]{1,2,0:T(8,128)S(1)}, f32[2,128,512]{1,2,0:T(8,128)S(1)}, u32[]{:S(2)}, u32[]{:S(2)}) collective-permute-start(f32[2,128,512]{1,2,0:T(8,128)S(1)} %get-tuple-element.22), channel_id=1, source_target_pairs={{0,32},{16,48},{32,0},{48,16},{64,96},{80,112},{96,64},{112,80},{1... | collective-permute-start | bytes 1572872 | tf_op jit(solution)/shard_map/ppermute | solution.py:16
  390.6 16.8 %collective-permute-start.14 = (f32[2,128,512]{1,2,0:T(8,128)S(1)}, f32[2,128,512]{1,2,0:T(8,128)S(1)}, u32[]{:S(2)}, u32[]{:S(2)}) collective-permute-start(f32[2,128,512]{1,2,0:T(8,128)S(1)} %get-tuple-element.21), channel_id=1, source_target_pairs={{0,64},{16,80},{32,96},{48,112},{64,0},{80,16},{96,32},{112,48},{1... | collective-permute-start | bytes 1572872 | tf_op jit(solution)/shard_map/ppermute | solution.py:16
  392.6 20.6 %collective-permute-start.15 = (f32[2,128,512]{1,2,0:T(8,128)S(1)}, f32[2,128,512]{1,2,0:T(8,128)}, u32[]{:S(2)}, u32[]{:S(2)}) collective-permute-start(f32[2,128,512]{1,2,0:T(8,128)S(1)} %get-tuple-element.20), channel_id=1, source_target_pairs={{0,64},{16,80},{32,96},{48,112},{64,0},{80,16},{96,32},{112,48},{1... | collective-permute-start | bytes 1572872 | tf_op jit(solution)/shard_map/ppermute | solution.py:16
  414.5 99.4 %collective-permute-start.16 = (f32[2,128,512]{1,2,0:T(8,128)S(1)}, f32[2,128,512]{1,2,0:T(8,128)S(1)}, u32[]{:S(2)}, u32[]{:S(2)}) collective-permute-start(f32[2,128,512]{1,2,0:T(8,128)S(1)} %get-tuple-element.19), channel_id=1, source_target_pairs={{0,128},{16,144},{32,160},{48,176},{64,192},{80,208},{96,224},{112... | collective-permute-start | bytes 1572872 | tf_op jit(solution)/shard_map/ppermute | solution.py:16
  420.0 93.9 %collective-permute-start.17 = (f32[2,128,512]{1,2,0:T(8,128)S(1)}, f32[2,128,512]{1,2,0:T(8,128)}, u32[]{:S(2)}, u32[]{:S(2)}) collective-permute-start(f32[2,128,512]{1,2,0:T(8,128)S(1)} %get-tuple-element.18), channel_id=1, source_target_pairs={{0,128},{16,144},{32,160},{48,176},{64,192},{80,208},{96,224},{112... | collective-permute-start | bytes 1572872 | tf_op jit(solution)/shard_map/ppermute | solution.py:16
  422.1 43.8 %collective-permute-start.24 = (bf16[128,512]{0,1:T(8,128)(2,1)S(1)}, bf16[128,512]{0,1:T(8,128)(2,1)S(1)}, u32[]{:S(2)}, u32[]{:S(2)}) collective-permute-start(bf16[128,512]{0,1:T(8,128)(2,1)S(1)} %copy.25), channel_id=1, source_target_pairs={{0,16},{16,32},{32,48},{48,64},{64,80},{80,96},{96,112},{112,128},... | collective-permute-start | bytes 393224 | tf_op jit(solution)/shard_map/ppermute | solution.py:22
  465.8 46.1 %collective-permute-start.25 = (bf16[128,512]{0,1:T(8,128)(2,1)S(1)}, bf16[128,512]{0,1:T(8,128)(2,1)}, u32[]{:S(2)}, u32[]{:S(2)}) collective-permute-start(bf16[128,512]{0,1:T(8,128)(2,1)S(1)} %collective-permute-done.24), channel_id=1, source_target_pairs={{0,16},{16,32},{32,48},{48,64},{64,80},{80,96},{96,112},{112,128},... | collective-permute-start | bytes 393224 | tf_op jit(solution)/shard_map/ppermute | solution.py:22
  512.0 13.6 %collective-permute-start.26 = (bf16[128,512]{0,1:T(8,128)(2,1)}, bf16[128,512]{0,1:T(8,128)(2,1)}, u32[]{:S(2)}, u32[]{:S(2)}) collective-permute-start(bf16[128,512]{0,1:T(8,128)(2,1)} %collective-permute-done.25), channel_id=1, source_target_pairs={{0,16},{16,32},{32,48},{48,64},{64,80},{80,96},{96,112},{112,128},... | collective-permute-start | bytes 393224 | tf_op jit(solution)/shard_map/ppermute | solution.py:22
  515.3 19.5 %collective-permute-start.18 = (f32[2,128,512]{1,2,0:T(8,128)S(1)}, f32[2,128,512]{1,2,0:T(8,128)S(1)}, u32[]{:S(2)}, u32[]{:S(2)}) collective-permute-start(f32[2,128,512]{1,2,0:T(8,128)S(1)} %get-tuple-element.17), channel_id=1, source_target_pairs={{0,256},{16,272},{32,288},{48,304},{64,320},{80,336},{96,352},{112... | collective-permute-start | bytes 1572872 | tf_op jit(solution)/shard_map/ppermute | solution.py:16
  519.6 20.3 %collective-permute-start.19 = (f32[2,128,512]{1,2,0:T(8,128)S(1)}, f32[2,128,512]{1,2,0:T(8,128)S(1)}, u32[]{:S(2)}, u32[]{:S(2)}) collective-permute-start(f32[2,128,512]{1,2,0:T(8,128)S(1)} %get-tuple-element.16), channel_id=1, source_target_pairs={{0,256},{16,272},{32,288},{48,304},{64,320},{80,336},{96,352},{112... | collective-permute-start | bytes 1572872 | tf_op jit(solution)/shard_map/ppermute | solution.py:16
  570.1 9.7 %collective-permute-start.20 = (bf16[128,512]{0,1:T(8,128)(2,1)S(1)}, bf16[128,512]{0,1:T(8,128)(2,1)S(1)}, u32[]{:S(2)}, u32[]{:S(2)}) collective-permute-start(bf16[128,512]{0,1:T(8,128)(2,1)S(1)} %fusion.14), channel_id=1, source_target_pairs={{0,16},{16,32},{32,48},{48,64},{64,80},{80,96},{96,112},{112,128},... | collective-permute-start | bytes 393224 | tf_op jit(solution)/shard_map/ppermute | solution.py:22
  (15 other events, 850.0 us)
where the time goes:
time: 609 us; the launch traced here: 608 us
  waiting for transfers between devices  448 us (74%)
  starting transfers between devices  88.8 us (15%)
  blocking collectives  29.7 us (5%)
  other arithmetic  19.3 us (3%)
  local copies, waits for them, and re-layouts  10.9 us (2%)
  matrix products  9.04 us (1%)
    ppermute x20, waiting for transfers between devices, swapped(): return lax.ppermute(value, axis, pairs)  332 us
    ppermute x8, waiting for transfers between devices, shifted(): return lax.ppermute(block, axis, route)  115 us
    ppermute x20, starting transfers between devices, swapped(): return lax.ppermute(value, axis, pairs)  72.1 us
    psum x1, blocking collectives, local(): row_power = lax.psum(jnp.sum(widened * widened, axis=1), 'mp')  29.7 us
    ppermute x8, starting transfers between devices, shifted(): return lax.ppermute(block, axis, route)  16.8 us
  transfers between devices with their start and end apart: 28, of which 23 were waited for; matrix products, arithmetic and copies ran while one was open for 1% of the time, Pallas kernels for 0%

commit v1 on v0

v1 whole, which is shorter than its diff:
```python
import functools
import math

import jax
import jax.numpy as jnp
import ml_dtypes
import numpy as np
from jax import lax
from jax.experimental import pallas as pl
from jax.experimental.pallas import tpu as pltpu
from jax.sharding import PartitionSpec as P

HEAD = 128
ROWS = 128
SPAN = 4
NX = 4
MESH = pl.DeviceIdType.MESH
F32 = jnp.float32
BF16 = jnp.bfloat16


def split(table):
    high = table.astype(np.float32).astype(ml_dtypes.bfloat16)
    low = (table - high.astype(np.float64)).astype(np.float32).astype(ml_dtypes.bfloat16)
    return high, low


def tables(blocks):
    length = blocks * ROWS
    n1 = np.arange(blocks)[None, :]
    k1 = np.arange(blocks)[:, None] + 0.25
    n2 = np.arange(ROWS)[None, :]
    first = np.exp(-2j * np.pi * n1 * k1 / blocks)
    twist = np.exp(-2j * np.pi * n2 * k1 / length)
    second = np.exp(-2j * np.pi * n2 * n2.T / ROWS)
    first_high, first_low = split(np.concatenate([first.real, first.imag], 0))
    first_cat = np.concatenate([first_high, first_low], 1)
    wide = np.block([[second.real, second.imag], [-second.imag, second.real]])
    wide_high, wide_low = split(wide)
    last_high, last_low = split(np.concatenate([first.real, first.imag], 0).T / length)
    last_cat = np.concatenate([last_high, last_low, last_high], 1)
    twists = np.stack([twist.real, twist.imag]).astype(np.float32)
    return first_cat, twists, wide_high, wide_low, last_cat


def halves(value):
    high = value.astype(BF16)
    return high, (value - high.astype(F32)).astype(BF16)


def kernel(
    blocks, n_mp, model,
    gate_ref, value_ref, out_gate_ref, taps_ref, query_ref, key_ref, skip_ref,
    first_ref, twist_ref, wide_high_ref, wide_low_ref, last_ref,
    mixer_ref, attended_ref,
    send_taps, send_signal, send_gate, recv_taps, recv_signal, work, spectrum,
    gate_head, query_head, key_head, back_send, back_recv, value_head, probs, denoms,
    power_mp, power_x, mixer_send, attended_send,
    send_sems, recv_sems,
):
    me = lax.axis_index("ctx")
    mp = lax.axis_index("mp")
    x, y = lax.rem(me, NX), lax.div(me, NX)
    n_y = blocks // NX
    width = NX * HEAD // blocks

    barrier = pltpu.get_barrier_semaphore()

    def greet_ctx(k, carry):
        pl.semaphore_signal(barrier, inc=1, device_id={"ctx": lax.rem(me + k, blocks)}, device_id_type=MESH)
        return carry

    def greet_mp(k, carry):
        pl.semaphore_signal(barrier, inc=1, device_id={"mp": lax.rem(mp + k, n_mp)}, device_id_type=MESH)
        return carry

    lax.fori_loop(1, blocks, greet_ctx, 0)
    lax.fori_loop(1, n_mp, greet_mp, 0)

    def send(src, dst, which, target):
        pltpu.make_async_remote_copy(
            src_ref=src, dst_ref=dst, send_sem=send_sems.at[which], recv_sem=recv_sems.at[which],
            device_id=target, device_id_type=MESH,
        ).start()

    def received(ref, which):
        pltpu.make_async_copy(ref, ref, recv_sems.at[which]).wait()

    def sent(ref, which):
        pltpu.make_async_copy(ref, ref, send_sems.at[which]).wait()

    def group(d):
        return pl.ds(pl.multiple_of(lax.rem(d, NX) * HEAD + lax.div(d, NX) * width, width), width)

    mine = pl.ds(pl.multiple_of(me * width, width), width)
    my_lanes = pl.ds(pl.multiple_of(x * HEAD, HEAD), HEAD)

    send_taps[...] = taps_ref[...].T.astype(BF16)
    send_signal[...] = (gate_ref[...].astype(F32) * value_ref[...].astype(F32)).T.astype(BF16)
    pl.semaphore_wait(barrier, blocks - 1 + n_mp - 1)

    def spread(which, src, dst):
        def step(k, carry):
            d = lax.rem(me + k, blocks)
            send(src.at[group(d)], dst.at[mine], which, {"ctx": d})
            return carry
        lax.fori_loop(1, blocks, step, 0)
        dst[mine] = src[group(me)]

    spread(0, send_taps, recv_taps)
    spread(1, send_signal, recv_signal)

    send_gate[...] = out_gate_ref[...].astype(F32).T.astype(BF16)
    own_rows = pl.ds(pl.multiple_of(SPAN * ROWS + x * ROWS, ROWS), ROWS)
    for k in range(1, NX):
        px = lax.rem(x + k, NX)
        target = {"ctx": y * NX + px}
        lanes = pl.ds(pl.multiple_of(px * HEAD, HEAD), HEAD)
        send(key_ref.at[:, lanes], key_head.at[own_rows], 2, target)
        send(query_ref.at[:, lanes], query_head.at[x], 3, target)
        send(send_gate.at[lanes], gate_head.at[x], 4, target)
    key_head[own_rows] = key_ref[:, my_lanes]
    query_head[x] = query_ref[:, my_lanes]
    gate_head[x] = send_gate[my_lanes]

    next_row = lax.rem(me + NX, blocks)
    received(key_head.at[pl.ds(0, (NX - 1) * ROWS)], 2)
    send(key_head.at[pl.ds(SPAN * ROWS, SPAN * ROWS)], key_head.at[pl.ds(0, SPAN * ROWS)], 5, {"ctx": next_row})

    twist_real, twist_imag = twist_ref[0], twist_ref[1]

    def times_wide(value, contract):
        high, low = halves(value)
        dims = (((1,), (contract,)), ((), ()))

        def dot(a, b):
            return lax.dot_general(a, b, dims, preferred_element_type=F32)

        return dot(high, wide_high_ref[...]) + dot(low, wide_high_ref[...]) + dot(high, wide_low_ref[...])

    def lane_tile(value, c):
        return value[:, c * ROWS:(c + 1) * ROWS]

    def forward(recv):
        work[...] = recv[...].astype(F32)
        panel = jnp.concatenate([work[pl.ds(c, blocks, stride=width), :] for c in range(width)], 1).astype(BF16)
        panel = jnp.concatenate([panel, panel], 0)
        bins = jnp.dot(first_ref[...], panel, preferred_element_type=F32)
        real, imag = bins[:blocks], bins[blocks:]
        rows = []
        for c in range(width):
            a, b = lane_tile(real, c), lane_tile(imag, c)
            rows.append(jnp.concatenate([a * twist_real - b * twist_imag, a * twist_imag + b * twist_real], 1))
        return times_wide(jnp.concatenate(rows, 0), 0)

    taps_rows = pl.ds(0, (blocks - 1) * width)
    received(recv_taps.at[taps_rows], 0)
    spectrum[...] = forward(recv_taps)
    skip_at = x * HEAD + y * width
    for c in range(width):
        rows = pl.ds(c * blocks, blocks)
        spectrum[rows, pl.ds(0, ROWS)] = spectrum[rows, pl.ds(0, ROWS)] + skip_ref[skip_at + c]
    received(recv_signal.at[taps_rows], 1)
    bins = forward(recv_signal)
    a, b = bins[:, :ROWS], bins[:, ROWS:]
    c, d = spectrum[:, pl.ds(0, ROWS)], spectrum[:, pl.ds(ROWS, ROWS)]
    back = times_wide(jnp.concatenate([a * c - b * d, a * d + b * c], 1), 1)
    columns = []
    for c in range(width):
        part = back[c * blocks:(c + 1) * blocks]
        a, b = part[:, :ROWS], part[:, ROWS:]
        columns.append(jnp.concatenate([a * twist_real + b * twist_imag, b * twist_real - a * twist_imag], 0))
    high, low = halves(jnp.concatenate(columns, 1))
    convolved = jnp.dot(last_ref[...], jnp.concatenate([high, high, low], 0), preferred_element_type=F32)
    for c in range(width):
        work[pl.ds(c, blocks, stride=width), :] = lane_tile(convolved, c)
    back_send[...] = work[...].astype(BF16).reshape(blocks, width, ROWS)
    for k in range(1, n_y):
        py = lax.rem(y + k, n_y)
        send(back_send.at[pl.ds(py * NX, NX)], back_recv.at[:, y], 6, {"ctx": py * NX + x})
    back_recv[:, y] = back_send[pl.ds(y * NX, NX)]

    received(query_head.at[pl.ds(0, NX - 1)], 3)
    received(key_head.at[pl.ds(0, SPAN * ROWS)], 5)
    reach = (SPAN + 1) * ROWS
    for j in range(NX):
        scores = lax.dot_general(
            key_head[pl.ds(j * ROWS, reach)], query_head[j], (((1,), (1,)), ((), ())), preferred_element_type=F32
        ) * (1.0 / math.sqrt(HEAD))
        key_at = lax.broadcasted_iota(jnp.int32, (reach, ROWS), 0)
        query_at = lax.broadcasted_iota(jnp.int32, (reach, ROWS), 1)
        first_key = jnp.where(y > 0, 0, SPAN * ROWS - j * ROWS)
        allowed = (key_at > query_at) & (key_at <= query_at + SPAN * ROWS) & (key_at >= first_key)
        scores = jnp.where(allowed, scores, -1e30)
        weights = jnp.exp(scores - jnp.max(scores, 0, keepdims=True))
        denoms[j] = jnp.broadcast_to(jnp.sum(weights, 0, keepdims=True), (8, ROWS))
        probs[j] = weights.astype(BF16)

    received(gate_head.at[pl.ds(0, NX - 1)], 4)
    received(back_send.at[pl.ds(0, (n_y - 1) * NX)], 6)
    gated = gate_head[...].astype(F32) * back_recv[...].reshape(NX, HEAD, ROWS).astype(F32)
    mixed = gated.astype(BF16)
    value_head[pl.ds(NX, NX)] = mixed
    send(value_head.at[pl.ds(NX, NX)], value_head.at[pl.ds(0, NX)], 7, {"ctx": next_row})
    widened = mixed.astype(F32)
    power = jnp.sum(widened * widened, 1)
    power_mp[mp] = jnp.concatenate([power, jnp.zeros_like(power)], 0)

    def share_power(k, carry):
        send(power_mp.at[mp], power_mp.at[mp], 8, {"mp": lax.rem(mp + k, n_mp)})
        return carry

    lax.fori_loop(1, n_mp, share_power, 0)

    for j in range(NX):
        mixer_send[j] = widened[j].T.astype(BF16)
    for k in range(1, NX):
        px = lax.rem(x + k, NX)
        send(mixer_send.at[px], mixer_ref.at[:, my_lanes], 9, {"ctx": y * NX + px})
    mixer_ref[:, my_lanes] = mixer_send[x]

    received(power_mp.at[pl.ds(0, n_mp - 1)], 8)
    power_x[NX + x] = jnp.sum(power_mp[...], 0)
    next_y = lax.rem(y + 1, n_y)
    for k in range(NX):
        px = lax.rem(x + k, NX)
        if k:
            send(power_x.at[NX + x], power_x.at[NX + x], 10, {"ctx": y * NX + px})
        send(power_x.at[NX + x], power_x.at[x], 11, {"ctx": next_y * NX + px})
    received(power_x.at[pl.ds(0, NX - 1)], 10)
    received(power_x.at[pl.ds(0, NX)], 11)
    received(value_head.at[pl.ds(0, NX)], 7)
    values = []
    for half in range(2):
        total = power_x[half * NX]
        for k in range(1, NX):
            total = total + power_x[half * NX + k]
        scale = lax.rsqrt(total * (1.0 / model) + 1e-06)
        for j in range(NX):
            values.append((value_head[half * NX + j].astype(F32) * scale[j:j + 1]).astype(BF16))
    for j in range(NX):
        summed = jnp.dot(jnp.concatenate(values[j:j + SPAN + 1], 1), probs[j], preferred_element_type=F32)
        attended_send[j] = (summed / denoms[j][0:1]).T.astype(BF16)
    for k in range(1, NX):
        px = lax.rem(x + k, NX)
        send(attended_send.at[px], attended_ref.at[:, my_lanes], 12, {"ctx": y * NX + px})
    attended_ref[:, my_lanes] = attended_send[x]

    sent(recv_taps.at[taps_rows], 0)
    sent(recv_signal.at[taps_rows], 1)
    sent(key_head.at[pl.ds(0, (NX - 1) * ROWS)], 2)
    sent(query_head.at[pl.ds(0, NX - 1)], 3)
    sent(gate_head.at[pl.ds(0, NX - 1)], 4)
    sent(key_head.at[pl.ds(0, SPAN * ROWS)], 5)
    sent(back_send.at[pl.ds(0, (n_y - 1) * NX)], 6)
    sent(value_head.at[pl.ds(0, NX)], 7)
    sent(power_mp.at[pl.ds(0, n_mp - 1)], 8)
    sent(mixer_send.at[pl.ds(0, NX - 1)], 9)
    sent(power_x.at[pl.ds(0, NX - 1)], 10)
    sent(power_x.at[pl.ds(0, NX)], 11)
    sent(attended_send.at[pl.ds(0, NX - 1)], 12)
    received(mixer_send.at[pl.ds(0, NX - 1)], 9)
    received(attended_send.at[pl.ds(0, NX - 1)], 12)


def solution(mesh):
    blocks, n_mp = mesh.shape["ctx"], mesh.shape["mp"]
    constants = tables(blocks)

    def local(gate_in, value_in, gate_out, filter_taps, skip_gain, queries, key_rows):
        rows, lanes = gate_in.shape
        width = lanes // blocks
        n_y = blocks // NX
        vmem = pl.BlockSpec(memory_space=pltpu.VMEM)
        square = (NX, ROWS, HEAD)
        return pl.pallas_call(
            functools.partial(kernel, blocks, n_mp, n_mp * lanes),
            out_shape=(jax.ShapeDtypeStruct((rows, lanes), BF16),) * 2,
            in_specs=[vmem] * 6 + [pl.BlockSpec(memory_space=pltpu.SMEM)] + [vmem] * 5,
            out_specs=(vmem, vmem),
            scratch_shapes=[
                pltpu.VMEM((lanes, ROWS), BF16),
                pltpu.VMEM((lanes, ROWS), BF16),
                pltpu.VMEM((lanes, ROWS), BF16),
                pltpu.VMEM((lanes, ROWS), BF16),
                pltpu.VMEM((lanes, ROWS), BF16),
                pltpu.VMEM((lanes, ROWS), F32),
                pltpu.VMEM((lanes, 2 * ROWS), F32),
                pltpu.VMEM(square, BF16),
                pltpu.VMEM(square, BF16),
                pltpu.VMEM((2 * SPAN * ROWS, HEAD), BF16),
                pltpu.VMEM((blocks, width, ROWS), BF16),
                pltpu.VMEM((NX, n_y, width, ROWS), BF16),
                pltpu.VMEM((2 * NX, HEAD, ROWS), BF16),
                pltpu.VMEM((NX, (SPAN + 1) * ROWS, ROWS), BF16),
                pltpu.VMEM((NX, 8, ROWS), F32),
                pltpu.VMEM((n_mp, 8, ROWS), F32),
                pltpu.VMEM((2 * NX, 8, ROWS), F32),
                pltpu.VMEM(square, BF16),
                pltpu.VMEM(square, BF16),
                pltpu.SemaphoreType.DMA((13,)),
                pltpu.SemaphoreType.DMA((13,)),
            ],
            compiler_params=pltpu.CompilerParams(
                collective_id=0, has_side_effects=True, vmem_limit_bytes=48 * 2**20
            ),
            cost_estimate=pl.CostEstimate(flops=2 * 10**9, bytes_accessed=2 * 10**6, transcendentals=4 * 10**5),
        )(gate_in, value_in, gate_out, filter_taps, queries, key_rows, skip_gain, *constants)

    return jax.shard_map(
        local,
        mesh=mesh,
        in_specs=(P("ctx", "mp"),) * 4 + (P("mp"),) + (P("ctx", "mp"),) * 2,
        out_specs=(P("ctx", "mp"), P("ctx", "mp")),
        check_vma=False,
    )
```

time: 609 us -> 58.9 us (0.10)
  the two profiles are of different devices: /device:TPU:16 before, /device:TPU:1 now
where the time goes in v1:
time: 58.9 us; the launch traced here: 58.1 us
  Pallas kernels  46 us (78%)
  local copies, waits for them, and re-layouts  11.5 us (20%)
  between operations  0.66 us (1%)
    pallas_call x1, Pallas kernels, local(): pl.pallas_call(functools.partial(kernel, blocks, n_mp, n_mp * lanes), out...  46 us
    unnamed x26, local copies, waits for them, and re-layouts  11.5 us

profile of v1, /device:TPU:1, one launch (start us, length us, event | category | flops | bytes accessed | tf_op | source)
XLA Modules:
  0.0 58.1 jit_solution(2257343884722413710)
XLA Ops:
  0.6 0.0 copy-start
  0.6 0.9 %copy-done = f32[128,512]{1,0:T(8,128)S(1)} copy-done((f32[128,512]{1,0:T(8,128)S(1)}, f32[128,512]{1,0:T(8,128)}, u32[]{:S(2)}) %copy-start) | copy-done | bytes 262168
  1.6 0.0 copy-start.1
  1.6 0.9 %copy-done.1 = bf16[128,512]{1,0:T(8,128)(2,1)S(1)} copy-done((bf16[128,512]{1,0:T(8,128)(2,1)S(1)}, bf16[128,512]{1,0:T(8,128)(2,1)}, u32[]{:S(2)}) %copy-start.1) | copy-done | bytes 131096
  2.5 0.0 copy-start.2
  2.5 0.9 %copy-done.2 = bf16[128,512]{1,0:T(8,128)(2,1)S(1)} copy-done((bf16[128,512]{1,0:T(8,128)(2,1)S(1)}, bf16[128,512]{1,0:T(8,128)(2,1)}, u32[]{:S(2)}) %copy-start.2) | copy-done | bytes 131096
  3.4 0.0 copy-start.3
  3.4 0.9 %copy-done.3 = bf16[128,512]{1,0:T(8,128)(2,1)S(1)} copy-done((bf16[128,512]{1,0:T(8,128)(2,1)S(1)}, bf16[128,512]{1,0:T(8,128)(2,1)}, u32[]{:S(2)}) %copy-start.3) | copy-done | bytes 131096
  4.3 0.0 copy-start.4
  4.3 0.9 %copy-done.4 = bf16[128,512]{1,0:T(8,128)(2,1)S(1)} copy-done((bf16[128,512]{1,0:T(8,128)(2,1)S(1)}, bf16[128,512]{1,0:T(8,128)(2,1)}, u32[]{:S(2)}) %copy-start.4) | copy-done | bytes 131096
  5.2 0.0 copy-start.5
  5.2 0.9 %copy-done.5 = bf16[128,512]{1,0:T(8,128)(2,1)S(1)} copy-done((bf16[128,512]{1,0:T(8,128)(2,1)S(1)}, bf16[128,512]{1,0:T(8,128)(2,1)}, u32[]{:S(2)}) %copy-start.5) | copy-done | bytes 131096
  6.1 0.0 copy-start.6
  6.1 0.7 %copy-done.6 = f32[512]{0:T(512)S(1)} copy-done((f32[512]{0:T(512)S(1)}, f32[512]{0:T(512)}, u32[]{:S(2)}) %copy-start.6) | copy-done | bytes 2072
  6.8 0.9 %copy-done.7 = bf16[256,256]{1,0:T(8,128)(2,1)S(1)} copy-done((bf16[256,256]{1,0:T(8,128)(2,1)S(1)}, bf16[256,256]{1,0:T(8,128)(2,1)}, u32[]{:S(2)}) %copy-start.7) | copy-done | bytes 131096
  7.7 0.0 copy-start.8
  7.7 0.9 %copy-done.8 = bf16[256,256]{1,0:T(8,128)(2,1)S(1)} copy-done((bf16[256,256]{1,0:T(8,128)(2,1)S(1)}, bf16[256,256]{1,0:T(8,128)(2,1)}, u32[]{:S(2)}) %copy-start.8) | copy-done | bytes 131096
  8.6 0.0 copy-start.9
  8.6 0.8 %copy-done.9 = f32[2,32,128]{2,1,0:T(8,128)S(1)} copy-done((f32[2,32,128]{2,1,0:T(8,128)S(1)}, f32[2,32,128]{2,1,0:T(8,128)}, u32[]{:S(2)}) %copy-start.9) | copy-done | bytes 32792
  9.4 0.7 %copy-done.10 = bf16[32,192]{1,0:T(8,128)(2,1)S(1)} copy-done((bf16[32,192]{1,0:T(8,128)(2,1)S(1)}, bf16[32,192]{1,0:T(8,128)(2,1)}, u32[]{:S(2)}) %copy-start.10) | copy-done | bytes 12312
  10.1 0.7 %copy-done.11 = bf16[64,64]{1,0:T(8,128)(2,1)S(1)} copy-done((bf16[64,64]{1,0:T(8,128)(2,1)S(1)}, bf16[64,64]{1,0:T(8,128)(2,1)}, u32[]{:S(2)}) %copy-start.11) | copy-done | bytes 8216
  10.8 46.0 %shard_map.131 = (bf16[128,512]{1,0:T(8,128)(2,1)S(1)}, bf16[128,512]{1,0:T(8,128)(2,1)S(1)}) custom-call(bf16[128,512]{1,0:T(8,128)(2,1)S(1)} %copy-done.1, bf16[128,512]{1,0:T(8,128)(2,1)S(1)} %copy-done.2, bf16[128,512]{1,0:T(8,128)(2,1)S(1)} %copy-done.3, f32[128,512]{1,0:T(8,128)S(1)} %copy-done, bf16[128,512]{1,0:T(8,128)(2,1)S(1)} %copy-done.4, ...), custom_call_target="tpu_custom_call" | custom-call | flops 2000000000 | bytes 2000000 | tf_op jit(solution)/shard_map/pallas_call | solution.py:276
  56.8 0.7 %copy.16 = bf16[128,512]{1,0:T(8,128)(2,1)} copy(bf16[128,512]{1,0:T(8,128)(2,1)S(1)} %get-tuple-element.4) | data formatting | bytes 262144
  57.5 0.7 %copy.17 = bf16[128,512]{1,0:T(8,128)(2,1)} copy(bf16[128,512]{1,0:T(8,128)(2,1)S(1)} %get-tuple-element.5) | data formatting | bytes 262144
  (3 shorter events, 0.0 us)
Async XLA Ops:
  0.6 1.0 %copy-start = (f32[128,512]{1,0:T(8,128)S(1)}, f32[128,512]{1,0:T(8,128)}, u32[]{:S(2)}) copy-start(f32[128,512]{1,0:T(8,128)} %taps_ref.1) | copy-start | bytes 786436
  1.6 0.9 %copy-start.1 = (bf16[128,512]{1,0:T(8,128)(2,1)S(1)}, bf16[128,512]{1,0:T(8,128)(2,1)}, u32[]{:S(2)}) copy-start(bf16[128,512]{1,0:T(8,128)(2,1)} %gate_ref.1) | copy-start | bytes 393220
  2.5 0.9 %copy-start.2 = (bf16[128,512]{1,0:T(8,128)(2,1)S(1)}, bf16[128,512]{1,0:T(8,128)(2,1)}, u32[]{:S(2)}) copy-start(bf16[128,512]{1,0:T(8,128)(2,1)} %value_ref.1) | copy-start | bytes 393220
  3.4 0.9 %copy-start.3 = (bf16[128,512]{1,0:T(8,128)(2,1)S(1)}, bf16[128,512]{1,0:T(8,128)(2,1)}, u32[]{:S(2)}) copy-start(bf16[128,512]{1,0:T(8,128)(2,1)} %out_gate_ref.1) | copy-start | bytes 393220
  4.3 0.9 %copy-start.4 = (bf16[128,512]{1,0:T(8,128)(2,1)S(1)}, bf16[128,512]{1,0:T(8,128)(2,1)}, u32[]{:S(2)}) copy-start(bf16[128,512]{1,0:T(8,128)(2,1)} %query_ref.1) | copy-start | bytes 393220
  5.2 0.9 %copy-start.5 = (bf16[128,512]{1,0:T(8,128)(2,1)S(1)}, bf16[128,512]{1,0:T(8,128)(2,1)}, u32[]{:S(2)}) copy-start(bf16[128,512]{1,0:T(8,128)(2,1)} %key_ref.1) | copy-start | bytes 393220
  6.1 0.7 %copy-start.6 = (f32[512]{0:T(512)S(1)}, f32[512]{0:T(512)}, u32[]{:S(2)}) copy-start(f32[512]{0:T(512)} %skip_ref.1) | copy-start | bytes 6148
  6.8 0.9 %copy-start.7 = (bf16[256,256]{1,0:T(8,128)(2,1)S(1)}, bf16[256,256]{1,0:T(8,128)(2,1)}, u32[]{:S(2)}) copy-start(bf16[256,256]{1,0:T(8,128)(2,1)} %constant.13.clone.wide_low_ref) | copy-start | bytes 393220
  7.7 0.9 %copy-start.8 = (bf16[256,256]{1,0:T(8,128)(2,1)S(1)}, bf16[256,256]{1,0:T(8,128)(2,1)}, u32[]{:S(2)}) copy-start(bf16[256,256]{1,0:T(8,128)(2,1)} %constant.12.clone.wide_high_ref) | copy-start | bytes 393220
  8.6 0.8 %copy-start.9 = (f32[2,32,128]{2,1,0:T(8,128)S(1)}, f32[2,32,128]{2,1,0:T(8,128)}, u32[]{:S(2)}) copy-start(f32[2,32,128]{2,1,0:T(8,128)} %constant.11.clone.twist_ref) | copy-start | bytes 98308
  9.4 0.7 %copy-start.10 = (bf16[32,192]{1,0:T(8,128)(2,1)S(1)}, bf16[32,192]{1,0:T(8,128)(2,1)}, u32[]{:S(2)}) copy-start(bf16[32,192]{1,0:T(8,128)(2,1)} %constant.14.clone.last_ref) | copy-start | bytes 36868
  10.1 0.7 %copy-start.11 = (bf16[64,64]{1,0:T(8,128)(2,1)S(1)}, bf16[64,64]{1,0:T(8,128)(2,1)}, u32[]{:S(2)}) copy-start(bf16[64,64]{1,0:T(8,128)(2,1)} %constant.10.clone.first_ref) | copy-start | bytes 24580

commit v2 on v1

--- a/solution.py
+++ b/solution.py
@@ -50,13 +50,15 @@
 
 def kernel(
     blocks, n_mp, model,
-    gate_ref, value_ref, out_gate_ref, taps_ref, query_ref, key_ref, skip_ref,
+    gate_hbm, value_hbm, out_gate_hbm, taps_hbm, query_hbm, key_hbm, skip_hbm,
+    first_hbm, twist_hbm, wide_high_hbm, wide_low_hbm, last_hbm,
+    mixer_hbm, attended_hbm,
+    gate_ref, value_ref, out_gate_ref, taps_ref, skip_ref,
     first_ref, twist_ref, wide_high_ref, wide_low_ref, last_ref,
-    mixer_ref, attended_ref,
     send_taps, send_signal, send_gate, recv_taps, recv_signal, work, spectrum,
     gate_head, query_head, key_head, back_send, back_recv, value_head, probs, denoms,
     power_mp, power_x, mixer_send, attended_send,
-    send_sems, recv_sems,
+    local_sems, send_sems, recv_sems,
 ):
     me = lax.axis_index("ctx")
     mp = lax.axis_index("mp")
@@ -64,6 +66,19 @@
     n_y = blocks // NX
     width = NX * HEAD // blocks
 
+    def fetch(src, dst, which):
+        copy = pltpu.make_async_copy(src, dst, local_sems.at[which])
+        copy.start()
+        return copy
+
+    loads = [
+        fetch(src, dst, which)
+        for which, (src, dst) in enumerate([
+            (taps_hbm, taps_ref), (gate_hbm, gate_ref), (value_hbm, value_ref), (out_gate_hbm, out_gate_ref),
+            (first_hbm, first_ref), (twist_hbm, twist_ref), (wide_high_hbm, wide_high_ref),
+            (wide_low_hbm, wide_low_ref), (last_hbm, last_ref), (skip_hbm, skip_ref),
+        ])
+    ]
     barrier = pltpu.get_barrier_semaphore()
 
     def greet_ctx(k, carry):
@@ -95,7 +110,10 @@
     mine = pl.ds(pl.multiple_of(me * width, width), width)
     my_lanes = pl.ds(pl.multiple_of(x * HEAD, HEAD), HEAD)
 
+    loads[0].wait()
     send_taps[...] = taps_ref[...].T.astype(BF16)
+    loads[1].wait()
+    loads[2].wait()
     send_signal[...] = (gate_ref[...].astype(F32) * value_ref[...].astype(F32)).T.astype(BF16)
     pl.semaphore_wait(barrier, blocks - 1 + n_mp - 1)
 
@@ -110,23 +128,27 @@
     spread(0, send_taps, recv_taps)
     spread(1, send_signal, recv_signal)
 
+    loads[3].wait()
     send_gate[...] = out_gate_ref[...].astype(F32).T.astype(BF16)
     own_rows = pl.ds(pl.multiple_of(SPAN * ROWS + x * ROWS, ROWS), ROWS)
     for k in range(1, NX):
         px = lax.rem(x + k, NX)
         target = {"ctx": y * NX + px}
         lanes = pl.ds(pl.multiple_of(px * HEAD, HEAD), HEAD)
-        send(key_ref.at[:, lanes], key_head.at[own_rows], 2, target)
-        send(query_ref.at[:, lanes], query_head.at[x], 3, target)
+        send(key_hbm.at[:, lanes], key_head.at[own_rows], 2, target)
+        send(query_hbm.at[:, lanes], query_head.at[x], 3, target)
         send(send_gate.at[lanes], gate_head.at[x], 4, target)
-    key_head[own_rows] = key_ref[:, my_lanes]
-    query_head[x] = query_ref[:, my_lanes]
+    own_key = fetch(key_hbm.at[:, my_lanes], key_head.at[own_rows], 10)
+    own_query = fetch(query_hbm.at[:, my_lanes], query_head.at[x], 11)
     gate_head[x] = send_gate[my_lanes]
 
     next_row = lax.rem(me + NX, blocks)
+    own_key.wait()
     received(key_head.at[pl.ds(0, (NX - 1) * ROWS)], 2)
     send(key_head.at[pl.ds(SPAN * ROWS, SPAN * ROWS)], key_head.at[pl.ds(0, SPAN * ROWS)], 5, {"ctx": next_row})
 
+    for load in loads[4:]:
+        load.wait()
     twist_real, twist_imag = twist_ref[0], twist_ref[1]
 
     def times_wide(value, contract):
@@ -180,6 +202,7 @@
         send(back_send.at[pl.ds(py * NX, NX)], back_recv.at[:, y], 6, {"ctx": py * NX + x})
     back_recv[:, y] = back_send[pl.ds(y * NX, NX)]
 
+    own_query.wait()
     received(query_head.at[pl.ds(0, NX - 1)], 3)
     received(key_head.at[pl.ds(0, SPAN * ROWS)], 5)
     reach = (SPAN + 1) * ROWS
@@ -216,8 +239,8 @@
         mixer_send[j] = widened[j].T.astype(BF16)
     for k in range(1, NX):
         px = lax.rem(x + k, NX)
-        send(mixer_send.at[px], mixer_ref.at[:, my_lanes], 9, {"ctx": y * NX + px})
-    mixer_ref[:, my_lanes] = mixer_send[x]
+        send(mixer_send.at[px], mixer_hbm.at[:, my_lanes], 9, {"ctx": y * NX + px})
+    own_mixer = fetch(mixer_send.at[x], mixer_hbm.at[:, my_lanes], 12)
 
     received(power_mp.at[pl.ds(0, n_mp - 1)], 8)
     power_x[NX + x] = jnp.sum(power_mp[...], 0)
@@ -243,8 +266,10 @@
         attended_send[j] = (summed / denoms[j][0:1]).T.astype(BF16)
     for k in range(1, NX):
         px = lax.rem(x + k, NX)
-        send(attended_send.at[px], attended_ref.at[:, my_lanes], 12, {"ctx": y * NX + px})
-    attended_ref[:, my_lanes] = attended_send[x]
+        send(attended_send.at[px], attended_hbm.at[:, my_lanes], 12, {"ctx": y * NX + px})
+    own_attended = fetch(attended_send.at[x], attended_hbm.at[:, my_lanes], 13)
+    own_mixer.wait()
+    own_attended.wait()
 
     sent(recv_taps.at[taps_rows], 0)
     sent(recv_signal.at[taps_rows], 1)
@@ -271,14 +296,20 @@
         rows, lanes = gate_in.shape
         width = lanes // blocks
         n_y = blocks // NX
-        vmem = pl.BlockSpec(memory_space=pltpu.VMEM)
+        hbm = pl.BlockSpec(memory_space=pltpu.HBM)
         square = (NX, ROWS, HEAD)
         return pl.pallas_call(
             functools.partial(kernel, blocks, n_mp, n_mp * lanes),
             out_shape=(jax.ShapeDtypeStruct((rows, lanes), BF16),) * 2,
-            in_specs=[vmem] * 6 + [pl.BlockSpec(memory_space=pltpu.SMEM)] + [vmem] * 5,
-            out_specs=(vmem, vmem),
+            in_specs=[hbm] * 12,
+            out_specs=(hbm, hbm),
             scratch_shapes=[
+                pltpu.VMEM((rows, lanes), BF16),
+                pltpu.VMEM((rows, lanes), BF16),
+                pltpu.VMEM((rows, lanes), BF16),
+                pltpu.VMEM((rows, lanes), F32),
+                pltpu.SMEM((lanes,), F32),
+                *(pltpu.VMEM(c.shape, c.dtype) for c in constants),
                 pltpu.VMEM((lanes, ROWS), BF16),
                 pltpu.VMEM((lanes, ROWS), BF16),
                 pltpu.VMEM((lanes, ROWS), BF16),
@@ -298,11 +329,12 @@
                 pltpu.VMEM((2 * NX, 8, ROWS), F32),
                 pltpu.VMEM(square, BF16),
                 pltpu.VMEM(square, BF16),
+                pltpu.SemaphoreType.DMA((14,)),
                 pltpu.SemaphoreType.DMA((13,)),
                 pltpu.SemaphoreType.DMA((13,)),
             ],
             compiler_params=pltpu.CompilerParams(
-                collective_id=0, has_side_effects=True, vmem_limit_bytes=48 * 2**20
+                collective_id=0, has_side_effects=True, vmem_limit_bytes=60 * 2**20
             ),
             cost_estimate=pl.CostEstimate(flops=2 * 10**9, bytes_accessed=2 * 10**6, transcendentals=4 * 10**5),
         )(gate_in, value_in, gate_out, filter_taps, queries, key_rows, skip_gain, *constants)

time: 58.9 us -> 49.2 us (0.84)
  local copies, waits for them, and re-layouts: 11.5 us -> 2.26 us
    unnamed x26 -> x4, local copies, waits for them, and re-layouts: 11.5 us -> 2.26 us
where the time goes in v2:
time: 49.2 us; the launch traced here: 48.7 us
  Pallas kernels  45.8 us (93%)
  local copies, waits for them, and re-layouts  2.26 us (5%)
  between operations  0.65 us (1%)
    pallas_call x1, Pallas kernels, local(): pl.pallas_call(functools.partial(kernel, blocks, n_mp, n_mp * lanes), out...  45.8 us
    unnamed x4, local copies, waits for them, and re-layouts  2.26 us

profile of v2, /device:TPU:1, one launch (start us, length us, event | category | flops | bytes accessed | tf_op | source)
XLA Modules:
  0.0 48.7 jit_solution(4219746850528910703)
XLA Ops:
  0.6 45.8 %shard_map.131 = (bf16[128,512]{1,0:T(8,128)(2,1)}, bf16[128,512]{1,0:T(8,128)(2,1)}) custom-call(bf16[128,512]{1,0:T(8,128)(2,1)} %gate_hbm.1, bf16[128,512]{1,0:T(8,128)(2,1)} %value_hbm.1, bf16[128,512]{1,0:T(8,128)(2,1)} %out_gate_hbm.1, f32[128,512]{1,0:T(8,128)} %taps_hbm.1, bf16[128,512]{1,0:T(8,128)(2,1)} %query_hbm.1, bf16[128,512]{1,0:T(8,128)(2,1)} %key_hbm.1, ...), custom_call_target="tpu_custom_call" | custom-call | flops 2000000000 | bytes 2000000 | tf_op jit(solution)/shard_map/pallas_call | solution.py:301
  46.5 0.0 copy-start
  46.5 1.6 %copy.16 = bf16[128,512]{1,0:T(8,128)(2,1)} copy(bf16[128,512]{1,0:T(8,128)(2,1)} %get-tuple-element.4) | data formatting | bytes 262144
  48.1 0.0 copy-done
  48.1 0.7 %copy.17 = bf16[128,512]{1,0:T(8,128)(2,1)} copy(bf16[128,512]{1,0:T(8,128)(2,1)S(1)} %copy-done) | data formatting | bytes 262144
Async XLA Ops:
  46.5 1.6 %copy-start = (bf16[128,512]{1,0:T(8,128)(2,1)S(1)}, bf16[128,512]{1,0:T(8,128)(2,1)}, u32[]{:S(2)}) copy-start(bf16[128,512]{1,0:T(8,128)(2,1)} %get-tuple-element.5) | copy-start | bytes 393220

commit v3 on v2

v3 whole, which is shorter than its diff:
```python
import functools
import math

import jax
import jax.numpy as jnp
import ml_dtypes
import numpy as np
from jax import lax
from jax.experimental import pallas as pl
from jax.experimental.pallas import tpu as pltpu
from jax.sharding import PartitionSpec as P

HEAD = 128
ROWS = 128
SPAN = 4
NX = 4
MESH = pl.DeviceIdType.MESH
F32 = jnp.float32
BF16 = jnp.bfloat16


def split(table):
    high = table.astype(np.float32).astype(ml_dtypes.bfloat16)
    low = (table - high.astype(np.float64)).astype(np.float32).astype(ml_dtypes.bfloat16)
    return high, low


def tables(blocks):
    length = blocks * ROWS
    n1 = np.arange(blocks)[None, :]
    k1 = np.arange(blocks)[:, None] + 0.25
    n2 = np.arange(ROWS)[None, :]
    first = np.exp(-2j * np.pi * n1 * k1 / blocks)
    twist = np.exp(-2j * np.pi * n2 * k1 / length)
    second = np.exp(-2j * np.pi * n2 * n2.T / ROWS)
    first_high, first_low = split(np.concatenate([first.real, first.imag], 0))
    first_cat = np.concatenate([first_high, first_low], 1)
    wide = np.block([[second.real, second.imag], [-second.imag, second.real]])
    wide_high, wide_low = split(wide)
    last_high, last_low = split(np.concatenate([first.real, first.imag], 0).T / length)
    last_cat = np.concatenate([last_high, last_low, last_high], 1)
    twists = np.stack([twist.real, twist.imag]).astype(np.float32)
    return first_cat, twists, wide_high, wide_low, last_cat


def halves(value):
    high = value.astype(BF16)
    return high, (value - high.astype(F32)).astype(BF16)


def kernel(
    blocks, n_mp, model,
    gate_hbm, value_hbm, out_gate_hbm, taps_hbm, query_hbm, key_hbm, skip_hbm,
    first_hbm, twist_hbm, wide_high_hbm, wide_low_hbm, last_hbm,
    mixer_hbm, attended_hbm,
    gate_ref, value_ref, out_gate_ref, taps_ref, query_ref, skip_ref,
    first_ref, twist_ref, wide_high_ref, wide_low_ref, last_ref,
    send_taps, send_signal, send_gate, recv_taps, recv_signal, work, spectrum,
    gate_head, back_send, back_recv, key_all, value_row, value_all, probs, denoms,
    power_x, power_mp, scales, mixer_out, attended_out,
    local_sems, send_sems, recv_sems,
):
    me = lax.axis_index("ctx")
    mp = lax.axis_index("mp")
    x, y = lax.rem(me, NX), lax.div(me, NX)
    n_y = blocks // NX
    width = NX * HEAD // blocks

    def far_first(k, count):
        half = lax.div(k + 1, 2)
        return lax.rem(count // 2 + jnp.where(lax.rem(k, 2) == 1, half, count - half), count)

    def ctx_peer(k):
        px = lax.rem(x + far_first(lax.rem(k, NX), NX), NX)
        py = lax.rem(y + far_first(lax.div(k, NX), n_y), n_y)
        return py * NX + px

    def mp_peer(k):
        return lax.rem(mp + far_first(k, n_mp), n_mp)

    barrier = pltpu.get_barrier_semaphore()

    def greet_ctx(k, carry):
        pl.semaphore_signal(barrier, inc=1, device_id={"ctx": ctx_peer(k)}, device_id_type=MESH)
        return carry

    def greet_mp(k, carry):
        pl.semaphore_signal(barrier, inc=1, device_id={"mp": mp_peer(k)}, device_id_type=MESH)
        return carry

    def fetch(src, dst, which):
        copy = pltpu.make_async_copy(src, dst, local_sems.at[which])
        copy.start()
        return copy

    first_loads = [
        fetch(src, dst, which)
        for which, (src, dst) in enumerate([(taps_hbm, taps_ref), (gate_hbm, gate_ref), (value_hbm, value_ref)])
    ]
    lax.fori_loop(0, blocks - 1, greet_ctx, 0)
    lax.fori_loop(0, n_mp - 1, greet_mp, 0)
    own_rows = pl.ds(SPAN * ROWS, ROWS)
    loads = [
        fetch(src, dst, 3 + which)
        for which, (src, dst) in enumerate([
            (out_gate_hbm, out_gate_ref), (first_hbm, first_ref), (twist_hbm, twist_ref),
            (wide_high_hbm, wide_high_ref), (wide_low_hbm, wide_low_ref), (last_hbm, last_ref), (skip_hbm, skip_ref),
            (query_hbm, query_ref), (key_hbm, key_all.at[own_rows]),
        ])
    ]

    def send(src, dst, which, target, send_which=None):
        pltpu.make_async_remote_copy(
            src_ref=src, dst_ref=dst, send_sem=send_sems.at[which if send_which is None else send_which],
            recv_sem=recv_sems.at[which], device_id=target, device_id_type=MESH,
        ).start()

    def received(ref, which):
        pltpu.make_async_copy(ref, ref, recv_sems.at[which]).wait()

    def sent(ref, which):
        pltpu.make_async_copy(ref, ref, send_sems.at[which]).wait()

    def group(d):
        return pl.ds(pl.multiple_of(lax.rem(d, NX) * HEAD + lax.div(d, NX) * width, width), width)

    mine = pl.ds(pl.multiple_of(me * width, width), width)
    my_lanes = pl.ds(pl.multiple_of(x * HEAD, HEAD), HEAD)

    first_loads[0].wait()
    send_taps[...] = taps_ref[...].T.astype(BF16)
    first_loads[1].wait()
    first_loads[2].wait()
    send_signal[...] = (gate_ref[...].astype(F32) * value_ref[...].astype(F32)).T.astype(BF16)
    pl.semaphore_wait(barrier, blocks - 1 + n_mp - 1)

    def spread(which, src, dst):
        def step(k, carry):
            d = ctx_peer(k)
            send(src.at[group(d)], dst.at[mine], which, {"ctx": d})
            return carry
        lax.fori_loop(0, blocks - 1, step, 0)
        dst[mine] = src[group(me)]

    spread(0, send_taps, recv_taps)
    spread(1, send_signal, recv_signal)

    loads[0].wait()
    send_gate[...] = out_gate_ref[...].astype(F32).T.astype(BF16)
    for k in (2, 1, 3):
        px = lax.rem(x + k, NX)
        lanes = pl.ds(pl.multiple_of(px * HEAD, HEAD), HEAD)
        send(send_gate.at[lanes], gate_head.at[x], 2, {"ctx": y * NX + px})
    gate_head[x] = send_gate[my_lanes]

    for load in loads[1:]:
        load.wait()
    twist_real, twist_imag = twist_ref[0], twist_ref[1]

    def times_wide(value, contract):
        high, low = halves(value)
        dims = (((1,), (contract,)), ((), ()))

        def dot(a, b):
            return lax.dot_general(a, b, dims, preferred_element_type=F32)

        return dot(high, wide_high_ref[...]) + dot(low, wide_high_ref[...]) + dot(high, wide_low_ref[...])

    def lane_tile(value, c):
        return value[:, c * ROWS:(c + 1) * ROWS]

    def forward(recv):
        work[...] = recv[...].astype(F32)
        panel = jnp.concatenate([work[pl.ds(c, blocks, stride=width), :] for c in range(width)], 1).astype(BF16)
        panel = jnp.concatenate([panel, panel], 0)
        bins = jnp.dot(first_ref[...], panel, preferred_element_type=F32)
        real, imag = bins[:blocks], bins[blocks:]
        rows = []
        for c in range(width):
            a, b = lane_tile(real, c), lane_tile(imag, c)
            rows.append(jnp.concatenate([a * twist_real - b * twist_imag, a * twist_imag + b * twist_real], 1))
        return times_wide(jnp.concatenate(rows, 0), 0)

    remote_rows = pl.ds(0, (blocks - 1) * width)
    received(recv_taps.at[remote_rows], 0)
    spectrum[...] = forward(recv_taps)
    skip_at = x * HEAD + y * width
    for c in range(width):
        rows = pl.ds(c * blocks, blocks)
        spectrum[rows, pl.ds(0, ROWS)] = spectrum[rows, pl.ds(0, ROWS)] + skip_ref[skip_at + c]
    received(recv_signal.at[remote_rows], 1)

    next_row = lax.rem(me + NX, blocks)
    own_keys, oldest_keys = key_all.at[own_rows], key_all.at[pl.ds(0, ROWS)]
    send(own_keys, oldest_keys, 3, {"ctx": next_row})
    for px in range(1, NX):
        @pl.when(x < px)
        def _():
            slot = pl.multiple_of((SPAN + x - px) * ROWS, ROWS)
            send(own_keys, key_all.at[pl.ds(slot, ROWS)], 4, {"ctx": y * NX + px})

    bins = forward(recv_signal)
    a, b = bins[:, :ROWS], bins[:, ROWS:]
    c, d = spectrum[:, pl.ds(0, ROWS)], spectrum[:, pl.ds(ROWS, ROWS)]
    back = times_wide(jnp.concatenate([a * c - b * d, a * d + b * c], 1), 1)
    columns = []
    for c in range(width):
        part = back[c * blocks:(c + 1) * blocks]
        a, b = part[:, :ROWS], part[:, ROWS:]
        columns.append(jnp.concatenate([a * twist_real + b * twist_imag, b * twist_real - a * twist_imag], 0))
    high, low = halves(jnp.concatenate(columns, 1))
    convolved = jnp.dot(last_ref[...], jnp.concatenate([high, high, low], 0), preferred_element_type=F32)
    for c in range(width):
        work[pl.ds(c, blocks, stride=width), :] = lane_tile(convolved, c)
    back_send[...] = work[...].astype(BF16).reshape(blocks, width, ROWS)

    def send_back(k, carry):
        py = lax.rem(y + far_first(k, n_y), n_y)
        send(back_send.at[pl.ds(py * NX, NX)], back_recv.at[:, y], 5, {"ctx": py * NX + x})
        return carry

    lax.fori_loop(0, n_y - 1, send_back, 0)
    back_recv[:, y] = back_send[pl.ds(y * NX, NX)]

    received(oldest_keys, 3)
    for px in range(NX - 1):
        @pl.when(x > px)
        def _():
            slot = pl.multiple_of((x - px) * ROWS, ROWS)
            send(oldest_keys, key_all.at[pl.ds(slot, ROWS)], 4, {"ctx": y * NX + px})

    received(gate_head.at[pl.ds(0, NX - 1)], 2)
    received(back_send.at[pl.ds(0, (n_y - 1) * NX)], 5)
    gated = gate_head[...].astype(F32) * back_recv[...].reshape(NX, HEAD, ROWS).astype(F32)
    mixed = gated.astype(BF16)
    value_row[...] = mixed
    widened = mixed.astype(F32)
    power = jnp.sum(widened * widened, 1)
    power_x[NX + x] = jnp.concatenate([power, jnp.zeros_like(power)], 0)
    next_y = lax.rem(y + 1, n_y)
    for k in (2, 1, 3, 0):
        px = lax.rem(x + k, NX)
        send(power_x.at[NX + x], power_x.at[x], 7, {"ctx": next_y * NX + px})
        if k:
            send(power_x.at[NX + x], power_x.at[NX + x], 6, {"ctx": y * NX + px})
    for px in range(NX):
        send(
            value_row.at[pl.ds(px, NX - px)], value_all.at[pl.ds(0, NX - px), x], 8 + x,
            {"ctx": next_y * NX + px}, 8,
        )
    for px in range(NX):
        src, dst = value_row.at[pl.ds(0, px + 1)], value_all.at[pl.ds(SPAN - px, px + 1), x]

        @pl.when(x != px)
        def _():
            send(src, dst, 8 + x, {"ctx": y * NX + px}, 9 + px)

        @pl.when(x == px)
        def _():
            pltpu.make_async_copy(src, dst, recv_sems.at[8 + x]).start()

    received(key_all.at[pl.ds(0, (NX - 1) * ROWS)], 4)
    reach = (SPAN + 1) * ROWS
    key_at = lax.broadcasted_iota(jnp.int32, (reach, ROWS), 0)
    query_at = lax.broadcasted_iota(jnp.int32, (reach, ROWS), 1)
    first_key = jnp.maximum(SPAN - me, 0) * ROWS
    allowed = (key_at > query_at) & (key_at <= query_at + SPAN * ROWS) & (key_at >= first_key)
    for h in range(NX):
        lanes = pl.ds(h * HEAD, HEAD)
        scores = lax.dot_general(
            key_all[:, lanes], query_ref[:, lanes], (((1,), (1,)), ((), ())), preferred_element_type=F32
        ) * (1.0 / math.sqrt(HEAD))
        scores = jnp.where(allowed, scores, -1e30)
        weights = jnp.exp(scores - jnp.max(scores, 0, keepdims=True))
        denoms[h] = jnp.broadcast_to(jnp.sum(weights, 0, keepdims=True), (8, ROWS))
        probs[h] = weights.astype(BF16)

    received(power_x.at[pl.ds(0, NX - 1)], 6)
    received(power_x.at[pl.ds(0, NX)], 7)
    totals = []
    for half in range(2):
        total = power_x[half * NX]
        for k in range(1, NX):
            total = total + power_x[half * NX + k]
        totals.append(total[:NX])
    power_mp[mp] = jnp.concatenate(totals, 0)

    def share_power(k, carry):
        send(power_mp.at[mp], power_mp.at[mp], 12, {"mp": mp_peer(k)}, 13)
        return carry

    lax.fori_loop(0, n_mp - 1, share_power, 0)

    for h in range(NX):
        received(value_all.at[:, h], 8 + h)
        mixer_out[:, pl.ds(h * HEAD, HEAD)] = value_all[SPAN, h].astype(F32).T.astype(BF16)
    mixer_copy = fetch(mixer_out, mixer_hbm, 12)

    received(power_mp.at[pl.ds(0, n_mp - 1)], 12)
    scales[...] = lax.rsqrt(jnp.sum(power_mp[...], 0) * (1.0 / model) + 1e-06)
    for h in range(NX):
        values = [
            (value_all[j, h].astype(F32) * scales[pl.ds(x + j, 1), :]).astype(BF16) for j in range(SPAN + 1)
        ]
        summed = jnp.dot(jnp.concatenate(values, 1), probs[h], preferred_element_type=F32)
        attended_out[:, pl.ds(h * HEAD, HEAD)] = (summed / denoms[h][0:1]).T.astype(BF16)
    attended_copy = fetch(attended_out, attended_hbm, 13)

    sent(recv_taps.at[remote_rows], 0)
    sent(recv_signal.at[remote_rows], 1)
    sent(gate_head.at[pl.ds(0, NX - 1)], 2)
    sent(oldest_keys, 3)
    sent(key_all.at[pl.ds(0, (NX - 1) * ROWS)], 4)
    sent(back_send.at[pl.ds(0, (n_y - 1) * NX)], 5)
    sent(power_x.at[pl.ds(0, NX - 1)], 6)
    sent(power_x.at[pl.ds(0, NX)], 7)
    sent(value_all.at[:, pl.ds(0, 2)], 8)
    for px in range(NX):
        @pl.when(x != px)
        def _():
            sent(value_row.at[pl.ds(0, px + 1)], 9 + px)
    sent(power_mp.at[pl.ds(0, n_mp - 1)], 13)
    mixer_copy.wait()
    attended_copy.wait()


def solution(mesh):
    blocks, n_mp = mesh.shape["ctx"], mesh.shape["mp"]
    constants = tables(blocks)

    def local(gate_in, value_in, gate_out, filter_taps, skip_gain, queries, key_rows):
        rows, lanes = gate_in.shape
        width = lanes // blocks
        n_y = blocks // NX
        hbm = pl.BlockSpec(memory_space=pltpu.HBM)
        square = (NX, ROWS, HEAD)
        return pl.pallas_call(
            functools.partial(kernel, blocks, n_mp, n_mp * lanes),
            out_shape=(jax.ShapeDtypeStruct((rows, lanes), BF16),) * 2,
            in_specs=[hbm] * 12,
            out_specs=(hbm, hbm),
            scratch_shapes=[
                *(pltpu.VMEM((rows, lanes), BF16),) * 3,
                pltpu.VMEM((rows, lanes), F32),
                pltpu.VMEM((rows, lanes), BF16),
                pltpu.SMEM((lanes,), F32),
                *(pltpu.VMEM(c.shape, c.dtype) for c in constants),
                *(pltpu.VMEM((lanes, ROWS), BF16),) * 5,
                pltpu.VMEM((lanes, ROWS), F32),
                pltpu.VMEM((lanes, 2 * ROWS), F32),
                pltpu.VMEM(square, BF16),
                pltpu.VMEM((blocks, width, ROWS), BF16),
                pltpu.VMEM((NX, n_y, width, ROWS), BF16),
                pltpu.VMEM(((SPAN + 1) * ROWS, lanes), BF16),
                pltpu.VMEM(square, BF16),
                pltpu.VMEM((SPAN + 1, NX, HEAD, ROWS), BF16),
                pltpu.VMEM((NX, (SPAN + 1) * ROWS, ROWS), BF16),
                pltpu.VMEM((NX, 8, ROWS), F32),
                pltpu.VMEM((2 * NX, 8, ROWS), F32),
                pltpu.VMEM((n_mp, 8, ROWS), F32),
                pltpu.VMEM((8, ROWS), F32),
                *(pltpu.VMEM((rows, lanes), BF16),) * 2,
                pltpu.SemaphoreType.DMA((14,)),
                pltpu.SemaphoreType.DMA((14,)),
                pltpu.SemaphoreType.DMA((13,)),
            ],
            compiler_params=pltpu.CompilerParams(
                collective_id=0, has_side_effects=True, vmem_limit_bytes=60 * 2**20
            ),
            cost_estimate=pl.CostEstimate(flops=2 * 10**9, bytes_accessed=2 * 10**6, transcendentals=4 * 10**5),
        )(gate_in, value_in, gate_out, filter_taps, queries, key_rows, skip_gain, *constants)

    return jax.shard_map(
        local,
        mesh=mesh,
        in_specs=(P("ctx", "mp"),) * 4 + (P("mp"),) + (P("ctx", "mp"),) * 2,
        out_specs=(P("ctx", "mp"), P("ctx", "mp")),
        check_vma=False,
    )
```

time: 49.2 us -> 52.7 us (1.071)
  Pallas kernels: 45.8 us -> 49.6 us
    pallas_call x1, Pallas kernels: 45.8 us -> 49.6 us  [local(): pl.pallas_call(functools.partial(kernel, blocks, n_mp, n_mp * lanes), out...]
where the time goes in v3:
time: 52.7 us; the launch traced here: 52.6 us
  Pallas kernels  49.6 us (94%)
  local copies, waits for them, and re-layouts  2.26 us (4%)
  between operations  0.65 us (1%)
    pallas_call x1, Pallas kernels, local(): pl.pallas_call(functools.partial(kernel, blocks, n_mp, n_mp * lanes), out...  49.6 us
    unnamed x4, local copies, waits for them, and re-layouts  2.26 us

profile of v3, /device:TPU:1, one launch (start us, length us, event | category | flops | bytes accessed | tf_op | source)
XLA Modules:
  0.0 52.6 jit_solution(9790962031645026528)
XLA Ops:
  0.6 49.6 %shard_map.131 = (bf16[128,512]{1,0:T(8,128)(2,1)}, bf16[128,512]{1,0:T(8,128)(2,1)}) custom-call(bf16[128,512]{1,0:T(8,128)(2,1)} %gate_hbm.1, bf16[128,512]{1,0:T(8,128)(2,1)} %value_hbm.1, bf16[128,512]{1,0:T(8,128)(2,1)} %out_gate_hbm.1, f32[128,512]{1,0:T(8,128)} %taps_hbm.1, bf16[128,512]{1,0:T(8,128)(2,1)} %query_hbm.1, bf16[128,512]{1,0:T(8,128)(2,1)} %key_hbm.1, ...), custom_call_target="tpu_custom_call" | custom-call | flops 2000000000 | bytes 2000000 | tf_op jit(solution)/shard_map/pallas_call | solution.py:337
  50.3 0.0 copy-start
  50.3 1.6 %copy.16 = bf16[128,512]{1,0:T(8,128)(2,1)} copy(bf16[128,512]{1,0:T(8,128)(2,1)} %get-tuple-element.4) | data formatting | bytes 262144
  51.9 0.0 copy-done
  51.9 0.7 %copy.17 = bf16[128,512]{1,0:T(8,128)(2,1)} copy(bf16[128,512]{1,0:T(8,128)(2,1)S(1)} %copy-done) | data formatting | bytes 262144
Async XLA Ops:
  50.3 1.6 %copy-start = (bf16[128,512]{1,0:T(8,128)(2,1)S(1)}, bf16[128,512]{1,0:T(8,128)(2,1)}, u32[]{:S(2)}) copy-start(bf16[128,512]{1,0:T(8,128)(2,1)} %get-tuple-element.5) | copy-start | bytes 393220

commit v4 on v3

--- a/solution.py
+++ b/solution.py
@@ -56,7 +56,7 @@
     gate_ref, value_ref, out_gate_ref, taps_ref, query_ref, skip_ref,
     first_ref, twist_ref, wide_high_ref, wide_low_ref, last_ref,
     send_taps, send_signal, send_gate, recv_taps, recv_signal, work, spectrum,
-    gate_head, back_send, back_recv, key_all, value_row, value_all, probs, denoms,
+    gate_head, back_send, back_recv, key_all, value_row, value_old, value_all, probs, denoms,
     power_x, power_mp, scales, mixer_out, attended_out,
     local_sems, send_sems, recv_sems,
 ):
@@ -145,6 +145,16 @@
     spread(0, send_taps, recv_taps)
     spread(1, send_signal, recv_signal)
 
+    loads[-1].wait()
+    next_row = lax.rem(me + NX, blocks)
+    own_keys, oldest_keys = key_all.at[own_rows], key_all.at[pl.ds(0, ROWS)]
+    send(own_keys, oldest_keys, 3, {"ctx": next_row})
+    for px in range(1, NX):
+        @pl.when(x < px)
+        def _():
+            slot = pl.multiple_of((SPAN + x - px) * ROWS, ROWS)
+            send(own_keys, key_all.at[pl.ds(slot, ROWS)], 4, {"ctx": y * NX + px})
+
     loads[0].wait()
     send_gate[...] = out_gate_ref[...].astype(F32).T.astype(BF16)
     for k in (2, 1, 3):
@@ -153,7 +163,7 @@
         send(send_gate.at[lanes], gate_head.at[x], 2, {"ctx": y * NX + px})
     gate_head[x] = send_gate[my_lanes]
 
-    for load in loads[1:]:
+    for load in loads[1:-1]:
         load.wait()
     twist_real, twist_imag = twist_ref[0], twist_ref[1]
 
@@ -189,15 +199,6 @@
         rows = pl.ds(c * blocks, blocks)
         spectrum[rows, pl.ds(0, ROWS)] = spectrum[rows, pl.ds(0, ROWS)] + skip_ref[skip_at + c]
     received(recv_signal.at[remote_rows], 1)
-
-    next_row = lax.rem(me + NX, blocks)
-    own_keys, oldest_keys = key_all.at[own_rows], key_all.at[pl.ds(0, ROWS)]
-    send(own_keys, oldest_keys, 3, {"ctx": next_row})
-    for px in range(1, NX):
-        @pl.when(x < px)
-        def _():
-            slot = pl.multiple_of((SPAN + x - px) * ROWS, ROWS)
-            send(own_keys, key_all.at[pl.ds(slot, ROWS)], 4, {"ctx": y * NX + px})
 
     bins = forward(recv_signal)
     a, b = bins[:, :ROWS], bins[:, ROWS:]
@@ -243,17 +244,41 @@
         send(power_x.at[NX + x], power_x.at[x], 7, {"ctx": next_y * NX + px})
         if k:
             send(power_x.at[NX + x], power_x.at[NX + x], 6, {"ctx": y * NX + px})
-    for px in range(NX):
-        send(
-            value_row.at[pl.ds(px, NX - px)], value_all.at[pl.ds(0, NX - px), x], 8 + x,
-            {"ctx": next_y * NX + px}, 8,
-        )
+    send(value_row, value_old, 13, {"ctx": next_row}, 8)
     for px in range(NX):
         src, dst = value_row.at[pl.ds(0, px + 1)], value_all.at[pl.ds(SPAN - px, px + 1), x]
 
         @pl.when(x != px)
         def _():
             send(src, dst, 8 + x, {"ctx": y * NX + px}, 9 + px)
+
+        @pl.when(x == px)
+        def _():
+            pltpu.make_async_copy(src, dst, recv_sems.at[8 + x]).start()
+
+    received(power_x.at[pl.ds(0, NX - 1)], 6)
+    received(power_x.at[pl.ds(0, NX)], 7)
+    totals = []
+    for half in range(2):
+        total = power_x[half * NX]
+        for k in range(1, NX):
+            total = total + power_x[half * NX + k]
+        totals.append(total[:NX])
+    power_mp[mp] = jnp.concatenate(totals, 0)
+
+    def share_power(k, carry):
+        send(power_mp.at[mp], power_mp.at[mp], 12, {"mp": mp_peer(k)}, 13)
+        return carry
+
+    lax.fori_loop(0, n_mp - 1, share_power, 0)
+
+    received(value_old, 13)
+    for px in range(NX):
+        src, dst = value_old.at[pl.ds(px, NX - px)], value_all.at[pl.ds(0, NX - px), x]
+
+        @pl.when(x != px)
+        def _():
+            send(src, dst, 8 + x, {"ctx": y * NX + px}, 14 + px)
 
         @pl.when(x == px)
         def _():
@@ -275,22 +300,6 @@
         denoms[h] = jnp.broadcast_to(jnp.sum(weights, 0, keepdims=True), (8, ROWS))
         probs[h] = weights.astype(BF16)
 
-    received(power_x.at[pl.ds(0, NX - 1)], 6)
-    received(power_x.at[pl.ds(0, NX)], 7)
-    totals = []
-    for half in range(2):
-        total = power_x[half * NX]
-        for k in range(1, NX):
-            total = total + power_x[half * NX + k]
-        totals.append(total[:NX])
-    power_mp[mp] = jnp.concatenate(totals, 0)
-
-    def share_power(k, carry):
-        send(power_mp.at[mp], power_mp.at[mp], 12, {"mp": mp_peer(k)}, 13)
-        return carry
-
-    lax.fori_loop(0, n_mp - 1, share_power, 0)
-
     for h in range(NX):
         received(value_all.at[:, h], 8 + h)
         mixer_out[:, pl.ds(h * HEAD, HEAD)] = value_all[SPAN, h].astype(F32).T.astype(BF16)
@@ -314,11 +323,12 @@
     sent(back_send.at[pl.ds(0, (n_y - 1) * NX)], 5)
     sent(power_x.at[pl.ds(0, NX - 1)], 6)
     sent(power_x.at[pl.ds(0, NX)], 7)
-    sent(value_all.at[:, pl.ds(0, 2)], 8)
+    sent(value_row, 8)
     for px in range(NX):
         @pl.when(x != px)
         def _():
             sent(value_row.at[pl.ds(0, px + 1)], 9 + px)
+            sent(value_row.at[pl.ds(0, NX - px)], 14 + px)
     sent(power_mp.at[pl.ds(0, n_mp - 1)], 13)
     mixer_copy.wait()
     attended_copy.wait()
@@ -353,6 +363,7 @@
                 pltpu.VMEM((NX, n_y, width, ROWS), BF16),
                 pltpu.VMEM(((SPAN + 1) * ROWS, lanes), BF16),
                 pltpu.VMEM(square, BF16),
+                pltpu.VMEM(square, BF16),
                 pltpu.VMEM((SPAN + 1, NX, HEAD, ROWS), BF16),
                 pltpu.VMEM((NX, (SPAN + 1) * ROWS, ROWS), BF16),
                 pltpu.VMEM((NX, 8, ROWS), F32),
@@ -361,8 +372,8 @@
                 pltpu.VMEM((8, ROWS), F32),
                 *(pltpu.VMEM((rows, lanes), BF16),) * 2,
                 pltpu.SemaphoreType.DMA((14,)),
+                pltpu.SemaphoreType.DMA((18,)),
                 pltpu.SemaphoreType.DMA((14,)),
-                pltpu.SemaphoreType.DMA((13,)),
             ],
             compiler_params=pltpu.CompilerParams(
                 collective_id=0, has_side_effects=True, vmem_limit_bytes=60 * 2**20

time: 52.7 us -> 45.2 us (0.86)
  Pallas kernels: 49.6 us -> 42.2 us
    pallas_call x1, Pallas kernels: 49.6 us -> 42.2 us  [local(): pl.pallas_call(functools.partial(kernel, blocks, n_mp, n_mp * lanes), out...]
where the time goes in v4:
time: 45.2 us; the launch traced here: 45.1 us
  Pallas kernels  42.2 us (93%)
  local copies, waits for them, and re-layouts  2.26 us (5%)
  between operations  0.65 us (1%)
    pallas_call x1, Pallas kernels, local(): pl.pallas_call(functools.partial(kernel, blocks, n_mp, n_mp * lanes), out...  42.2 us
    unnamed x4, local copies, waits for them, and re-layouts  2.26 us

profile of v4, /device:TPU:1, one launch (start us, length us, event | category | flops | bytes accessed | tf_op | source)
XLA Modules:
  0.0 45.1 jit_solution(11136120963899749398)
XLA Ops:
  0.6 42.2 %shard_map.131 = (bf16[128,512]{1,0:T(8,128)(2,1)}, bf16[128,512]{1,0:T(8,128)(2,1)}) custom-call(bf16[128,512]{1,0:T(8,128)(2,1)} %gate_hbm.1, bf16[128,512]{1,0:T(8,128)(2,1)} %value_hbm.1, bf16[128,512]{1,0:T(8,128)(2,1)} %out_gate_hbm.1, f32[128,512]{1,0:T(8,128)} %taps_hbm.1, bf16[128,512]{1,0:T(8,128)(2,1)} %query_hbm.1, bf16[128,512]{1,0:T(8,128)(2,1)} %key_hbm.1, ...), custom_call_target="tpu_custom_call" | custom-call | flops 2000000000 | bytes 2000000 | tf_op jit(solution)/shard_map/pallas_call | solution.py:347
  42.8 0.0 copy-start
  42.8 1.6 %copy.16 = bf16[128,512]{1,0:T(8,128)(2,1)} copy(bf16[128,512]{1,0:T(8,128)(2,1)} %get-tuple-element.4) | data formatting | bytes 262144
  44.5 0.0 copy-done
  44.5 0.7 %copy.17 = bf16[128,512]{1,0:T(8,128)(2,1)} copy(bf16[128,512]{1,0:T(8,128)(2,1)S(1)} %copy-done) | data formatting | bytes 262144
Async XLA Ops:
  42.8 1.6 %copy-start = (bf16[128,512]{1,0:T(8,128)(2,1)S(1)}, bf16[128,512]{1,0:T(8,128)(2,1)}, u32[]{:S(2)}) copy-start(bf16[128,512]{1,0:T(8,128)(2,1)} %get-tuple-element.5) | copy-start | bytes 393220

commit v5 on v4

--- a/solution.py
+++ b/solution.py
@@ -52,12 +52,12 @@
     blocks, n_mp, model,
     gate_hbm, value_hbm, out_gate_hbm, taps_hbm, query_hbm, key_hbm, skip_hbm,
     first_hbm, twist_hbm, wide_high_hbm, wide_low_hbm, last_hbm,
-    mixer_hbm, attended_hbm,
+    mixer_out, attended_out,
     gate_ref, value_ref, out_gate_ref, taps_ref, query_ref, skip_ref,
     first_ref, twist_ref, wide_high_ref, wide_low_ref, last_ref,
     send_taps, send_signal, send_gate, recv_taps, recv_signal, work, spectrum,
     gate_head, back_send, back_recv, key_all, value_row, value_old, value_all, probs, denoms,
-    power_x, power_mp, scales, mixer_out, attended_out,
+    power_x, power_mp, scales,
     local_sems, send_sems, recv_sems,
 ):
     me = lax.axis_index("ctx")
@@ -303,7 +303,6 @@
     for h in range(NX):
         received(value_all.at[:, h], 8 + h)
         mixer_out[:, pl.ds(h * HEAD, HEAD)] = value_all[SPAN, h].astype(F32).T.astype(BF16)
-    mixer_copy = fetch(mixer_out, mixer_hbm, 12)
 
     received(power_mp.at[pl.ds(0, n_mp - 1)], 12)
     scales[...] = lax.rsqrt(jnp.sum(power_mp[...], 0) * (1.0 / model) + 1e-06)
@@ -313,7 +312,6 @@
         ]
         summed = jnp.dot(jnp.concatenate(values, 1), probs[h], preferred_element_type=F32)
         attended_out[:, pl.ds(h * HEAD, HEAD)] = (summed / denoms[h][0:1]).T.astype(BF16)
-    attended_copy = fetch(attended_out, attended_hbm, 13)
 
     sent(recv_taps.at[remote_rows], 0)
     sent(recv_signal.at[remote_rows], 1)
@@ -330,8 +328,17 @@
             sent(value_row.at[pl.ds(0, px + 1)], 9 + px)
             sent(value_row.at[pl.ds(0, NX - px)], 14 + px)
     sent(power_mp.at[pl.ds(0, n_mp - 1)], 13)
-    mixer_copy.wait()
-    attended_copy.wait()
+
+
+def hand_over(mixer_from, attended_from, mixer_to, attended_to, sems):
+    copies = [
+        pltpu.make_async_copy(mixer_from, mixer_to, sems.at[0]),
+        pltpu.make_async_copy(attended_from, attended_to, sems.at[1]),
+    ]
+    for copy in copies:
+        copy.start()
+    for copy in copies:
+        copy.wait()
 
 
 def solution(mesh):
@@ -344,11 +351,13 @@
         n_y = blocks // NX
         hbm = pl.BlockSpec(memory_space=pltpu.HBM)
         square = (NX, ROWS, HEAD)
-        return pl.pallas_call(
+        operands = gate_in, value_in, gate_out, filter_taps, queries, key_rows, skip_gain, *constants
+        operands = [pltpu.with_memory_space_constraint(o, pltpu.HBM) for o in operands]
+        mixer, attended = pl.pallas_call(
             functools.partial(kernel, blocks, n_mp, n_mp * lanes),
-            out_shape=(jax.ShapeDtypeStruct((rows, lanes), BF16),) * 2,
+            out_shape=(pltpu.VMEM((rows, lanes), BF16),) * 2,
             in_specs=[hbm] * 12,
-            out_specs=(hbm, hbm),
+            out_specs=(pl.BlockSpec(memory_space=pltpu.VMEM),) * 2,
             scratch_shapes=[
                 *(pltpu.VMEM((rows, lanes), BF16),) * 3,
                 pltpu.VMEM((rows, lanes), F32),
@@ -370,16 +379,23 @@
                 pltpu.VMEM((2 * NX, 8, ROWS), F32),
                 pltpu.VMEM((n_mp, 8, ROWS), F32),
                 pltpu.VMEM((8, ROWS), F32),
-                *(pltpu.VMEM((rows, lanes), BF16),) * 2,
                 pltpu.SemaphoreType.DMA((14,)),
                 pltpu.SemaphoreType.DMA((18,)),
                 pltpu.SemaphoreType.DMA((14,)),
             ],
             compiler_params=pltpu.CompilerParams(
-                collective_id=0, has_side_effects=True, vmem_limit_bytes=60 * 2**20
+                collective_id=0, has_side_effects=True, vmem_limit_bytes=32 * 2**20
             ),
             cost_estimate=pl.CostEstimate(flops=2 * 10**9, bytes_accessed=2 * 10**6, transcendentals=4 * 10**5),
-        )(gate_in, value_in, gate_out, filter_taps, queries, key_rows, skip_gain, *constants)
+        )(*operands)
+        return pl.pallas_call(
+            hand_over,
+            out_shape=(jax.ShapeDtypeStruct((rows, lanes), BF16),) * 2,
+            in_specs=[pl.BlockSpec(memory_space=pltpu.VMEM)] * 2,
+            out_specs=(hbm,) * 2,
+            scratch_shapes=[pltpu.SemaphoreType.DMA((2,))],
+            compiler_params=pltpu.CompilerParams(vmem_limit_bytes=8 * 2**20),
+        )(mixer, attended)
 
     return jax.shard_map(
         local,

time: 45.2 us -> 43.1 us (0.954)
  local copies, waits for them, and re-layouts: 2.26 us -> 0 us
    unnamed x4 -> x0, local copies, waits for them, and re-layouts: 2.26 us -> none
    pallas_call x0 -> x1, Pallas kernels: none -> 0.72 us  [local(): pl.pallas_call(hand_over, out_shape=(jax.ShapeDtypeStruct((rows, lanes),...]
    pallas_call x1, Pallas kernels: 42.2 us -> 41.7 us  [local(): pl.pallas_call(functools.partial(kernel, blocks, n_mp, n_mp * lanes), out...]
where the time goes in v5:
time: 43.1 us; the launch traced here: 43 us
  Pallas kernels  42.4 us (98%)
  between operations  0.64 us (1%)
    pallas_call x1, Pallas kernels, local(): pl.pallas_call(functools.partial(kernel, blocks, n_mp, n_mp * lanes), out...  41.7 us

profile of v5, /device:TPU:1, one launch (start us, length us, event | category | flops | bytes accessed | tf_op | source)
XLA Modules:
  0.0 43.0 jit_solution(16648075691015880981)
XLA Ops:
  0.6 41.7 %shard_map.131 = (bf16[128,512]{1,0:T(8,128)(2,1)S(1)}, bf16[128,512]{1,0:T(8,128)(2,1)S(1)}) custom-call(bf16[128,512]{1,0:T(8,128)(2,1)} %gate_hbm.1, bf16[128,512]{1,0:T(8,128)(2,1)} %value_hbm.1, bf16[128,512]{1,0:T(8,128)(2,1)} %out_gate_hbm.1, f32[128,512]{1,0:T(8,128)} %taps_hbm.1, bf16[128,512]{1,0:T(8,128)(2,1)} %query_hbm.1, ...), custom_call_target="tpu_custom_call" | custom-call | flops 2000000000 | bytes 2000000 | tf_op jit(solution)/shard_map/pallas_call | solution.py:356
  42.3 0.7 %shard_map.132 = (bf16[128,512]{1,0:T(8,128)(2,1)}, bf16[128,512]{1,0:T(8,128)(2,1)}) custom-call(bf16[128,512]{1,0:T(8,128)(2,1)S(1)} %get-tuple-element.4.mixer_from, bf16[128,512]{1,0:T(8,128)(2,1)S(1)} %get-tuple-element.5.attended_from), custom_call_target="tpu_custom_call" | custom-call | tf_op jit(solution)/shard_map/pallas_call | solution.py:391

commit v6 on v5

--- a/solution.py
+++ b/solution.py
@@ -148,12 +148,20 @@
     loads[-1].wait()
     next_row = lax.rem(me + NX, blocks)
     own_keys, oldest_keys = key_all.at[own_rows], key_all.at[pl.ds(0, ROWS)]
-    send(own_keys, oldest_keys, 3, {"ctx": next_row})
+    @pl.when(y < n_y - 1)
+    def _():
+        send(own_keys, oldest_keys, 3, {"ctx": next_row})
+
     for px in range(1, NX):
         @pl.when(x < px)
         def _():
             slot = pl.multiple_of((SPAN + x - px) * ROWS, ROWS)
             send(own_keys, key_all.at[pl.ds(slot, ROWS)], 4, {"ctx": y * NX + px})
+
+    @pl.when(y == 0)
+    def _():
+        value_old[...] = jnp.zeros_like(value_old)
+        power_x[pl.ds(0, NX)] = jnp.zeros((NX, 8, ROWS), F32)
 
     loads[0].wait()
     send_gate[...] = out_gate_ref[...].astype(F32).T.astype(BF16)
@@ -223,7 +231,10 @@
     lax.fori_loop(0, n_y - 1, send_back, 0)
     back_recv[:, y] = back_send[pl.ds(y * NX, NX)]
 
-    received(oldest_keys, 3)
+    @pl.when(y > 0)
+    def _():
+        received(oldest_keys, 3)
+
     for px in range(NX - 1):
         @pl.when(x > px)
         def _():
@@ -241,10 +252,18 @@
     next_y = lax.rem(y + 1, n_y)
     for k in (2, 1, 3, 0):
         px = lax.rem(x + k, NX)
-        send(power_x.at[NX + x], power_x.at[x], 7, {"ctx": next_y * NX + px})
+
+        @pl.when(y < n_y - 1)
+        def _():
+            send(power_x.at[NX + x], power_x.at[x], 7, {"ctx": next_y * NX + px})
+
         if k:
             send(power_x.at[NX + x], power_x.at[NX + x], 6, {"ctx": y * NX + px})
-    send(value_row, value_old, 13, {"ctx": next_row}, 8)
+
+    @pl.when(y < n_y - 1)
+    def _():
+        send(value_row, value_old, 13, {"ctx": next_row}, 8)
+
     for px in range(NX):
         src, dst = value_row.at[pl.ds(0, px + 1)], value_all.at[pl.ds(SPAN - px, px + 1), x]
 
@@ -257,7 +276,11 @@
             pltpu.make_async_copy(src, dst, recv_sems.at[8 + x]).start()
 
     received(power_x.at[pl.ds(0, NX - 1)], 6)
-    received(power_x.at[pl.ds(0, NX)], 7)
+
+    @pl.when(y > 0)
+    def _():
+        received(power_x.at[pl.ds(0, NX)], 7)
+
     totals = []
     for half in range(2):
         total = power_x[half * NX]
@@ -272,7 +295,10 @@
 
     lax.fori_loop(0, n_mp - 1, share_power, 0)
 
-    received(value_old, 13)
+    @pl.when(y > 0)
+    def _():
+        received(value_old, 13)
+
     for px in range(NX):
         src, dst = value_old.at[pl.ds(px, NX - px)], value_all.at[pl.ds(0, NX - px), x]
 
@@ -316,12 +342,15 @@
     sent(recv_taps.at[remote_rows], 0)
     sent(recv_signal.at[remote_rows], 1)
     sent(gate_head.at[pl.ds(0, NX - 1)], 2)
-    sent(oldest_keys, 3)
+    @pl.when(y < n_y - 1)
+    def _():
+        sent(oldest_keys, 3)
+        sent(power_x.at[pl.ds(0, NX)], 7)
+        sent(value_row, 8)
+
     sent(key_all.at[pl.ds(0, (NX - 1) * ROWS)], 4)
     sent(back_send.at[pl.ds(0, (n_y - 1) * NX)], 5)
     sent(power_x.at[pl.ds(0, NX - 1)], 6)
-    sent(power_x.at[pl.ds(0, NX)], 7)
-    sent(value_row, 8)
     for px in range(NX):
         @pl.when(x != px)
         def _():

time: 43.1 us -> 42.9 us (level)
  no operation moved by 1% of the time
where the time goes in v6:
time: 42.9 us; the launch traced here: 42.8 us
  Pallas kernels  42.1 us (98%)
  between operations  0.64 us (1%)
    pallas_call x1, Pallas kernels, local(): pl.pallas_call(functools.partial(kernel, blocks, n_mp, n_mp * lanes), out...  41.4 us

profile of v6, /device:TPU:1, one launch (start us, length us, event | category | flops | bytes accessed | tf_op | source)
XLA Modules:
  0.0 42.8 jit_solution(4193969884796390276)
XLA Ops:
  0.6 41.4 %shard_map.131 = (bf16[128,512]{1,0:T(8,128)(2,1)S(1)}, bf16[128,512]{1,0:T(8,128)(2,1)S(1)}) custom-call(bf16[128,512]{1,0:T(8,128)(2,1)} %gate_hbm.1, bf16[128,512]{1,0:T(8,128)(2,1)} %value_hbm.1, bf16[128,512]{1,0:T(8,128)(2,1)} %out_gate_hbm.1, f32[128,512]{1,0:T(8,128)} %taps_hbm.1, bf16[128,512]{1,0:T(8,128)(2,1)} %query_hbm.1, ...), custom_call_target="tpu_custom_call" | custom-call | flops 2000000000 | bytes 2000000 | tf_op jit(solution)/shard_map/pallas_call | solution.py:385
  42.0 0.7 %shard_map.132 = (bf16[128,512]{1,0:T(8,128)(2,1)}, bf16[128,512]{1,0:T(8,128)(2,1)}) custom-call(bf16[128,512]{1,0:T(8,128)(2,1)S(1)} %get-tuple-element.4.mixer_from, bf16[128,512]{1,0:T(8,128)(2,1)S(1)} %get-tuple-element.5.attended_from), custom_call_target="tpu_custom_call" | custom-call | tf_op jit(solution)/shard_map/pallas_call | solution.py:420

commit v7 on v6

--- a/solution.py
+++ b/solution.py
@@ -52,12 +52,12 @@
     blocks, n_mp, model,
     gate_hbm, value_hbm, out_gate_hbm, taps_hbm, query_hbm, key_hbm, skip_hbm,
     first_hbm, twist_hbm, wide_high_hbm, wide_low_hbm, last_hbm,
-    mixer_out, attended_out,
+    mixer_out, value_all, probs, denoms, scales,
     gate_ref, value_ref, out_gate_ref, taps_ref, query_ref, skip_ref,
     first_ref, twist_ref, wide_high_ref, wide_low_ref, last_ref,
     send_taps, send_signal, send_gate, recv_taps, recv_signal, work, spectrum,
-    gate_head, back_send, back_recv, key_all, value_row, value_old, value_all, probs, denoms,
-    power_x, power_mp, scales,
+    gate_head, back_send, back_recv, key_all, value_row, value_old,
+    power_x, power_mp,
     local_sems, send_sems, recv_sems,
 ):
     me = lax.axis_index("ctx")
@@ -332,40 +332,40 @@
 
     received(power_mp.at[pl.ds(0, n_mp - 1)], 12)
     scales[...] = lax.rsqrt(jnp.sum(power_mp[...], 0) * (1.0 / model) + 1e-06)
+
+    sent(recv_taps.at[remote_rows], 0)
+    sent(recv_signal.at[remote_rows], 1)
+    sent(gate_head.at[pl.ds(0, NX - 1)], 2)
+    @pl.when(y < n_y - 1)
+    def _():
+        sent(oldest_keys, 3)
+        sent(power_x.at[pl.ds(0, NX)], 7)
+        sent(value_row, 8)
+
+    sent(key_all.at[pl.ds(0, (NX - 1) * ROWS)], 4)
+    sent(back_send.at[pl.ds(0, (n_y - 1) * NX)], 5)
+    sent(power_x.at[pl.ds(0, NX - 1)], 6)
+    for px in range(NX):
+        @pl.when(x != px)
+        def _():
+            sent(value_row.at[pl.ds(0, px + 1)], 9 + px)
+            sent(value_row.at[pl.ds(0, NX - px)], 14 + px)
+    sent(power_mp.at[pl.ds(0, n_mp - 1)], 13)
+
+
+def attend(mixer_from, value_all, probs, denoms, scales, mixer_to, attended_to, attended, sems):
+    x = lax.rem(lax.axis_index("ctx"), NX)
+    copies = [pltpu.make_async_copy(mixer_from, mixer_to, sems.at[NX])]
+    copies[0].start()
     for h in range(NX):
         values = [
             (value_all[j, h].astype(F32) * scales[pl.ds(x + j, 1), :]).astype(BF16) for j in range(SPAN + 1)
         ]
         summed = jnp.dot(jnp.concatenate(values, 1), probs[h], preferred_element_type=F32)
-        attended_out[:, pl.ds(h * HEAD, HEAD)] = (summed / denoms[h][0:1]).T.astype(BF16)
-
-    sent(recv_taps.at[remote_rows], 0)
-    sent(recv_signal.at[remote_rows], 1)
-    sent(gate_head.at[pl.ds(0, NX - 1)], 2)
-    @pl.when(y < n_y - 1)
-    def _():
-        sent(oldest_keys, 3)
-        sent(power_x.at[pl.ds(0, NX)], 7)
-        sent(value_row, 8)
-
-    sent(key_all.at[pl.ds(0, (NX - 1) * ROWS)], 4)
-    sent(back_send.at[pl.ds(0, (n_y - 1) * NX)], 5)
-    sent(power_x.at[pl.ds(0, NX - 1)], 6)
-    for px in range(NX):
-        @pl.when(x != px)
-        def _():
-            sent(value_row.at[pl.ds(0, px + 1)], 9 + px)
-            sent(value_row.at[pl.ds(0, NX - px)], 14 + px)
-    sent(power_mp.at[pl.ds(0, n_mp - 1)], 13)
-
-
-def hand_over(mixer_from, attended_from, mixer_to, attended_to, sems):
-    copies = [
-        pltpu.make_async_copy(mixer_from, mixer_to, sems.at[0]),
-        pltpu.make_async_copy(attended_from, attended_to, sems.at[1]),
-    ]
-    for copy in copies:
-        copy.start()
+        lanes = pl.ds(h * HEAD, HEAD)
+        attended[:, lanes] = (summed / denoms[h][0:1]).T.astype(BF16)
+        copies.append(pltpu.make_async_copy(attended.at[:, lanes], attended_to.at[:, lanes], sems.at[h]))
+        copies[-1].start()
     for copy in copies:
         copy.wait()
 
@@ -382,11 +382,17 @@
         square = (NX, ROWS, HEAD)
         operands = gate_in, value_in, gate_out, filter_taps, queries, key_rows, skip_gain, *constants
         operands = [pltpu.with_memory_space_constraint(o, pltpu.HBM) for o in operands]
-        mixer, attended = pl.pallas_call(
+        held = pl.pallas_call(
             functools.partial(kernel, blocks, n_mp, n_mp * lanes),
-            out_shape=(pltpu.VMEM((rows, lanes), BF16),) * 2,
+            out_shape=(
+                pltpu.VMEM((rows, lanes), BF16),
+                pltpu.VMEM((SPAN + 1, NX, HEAD, ROWS), BF16),
+                pltpu.VMEM((NX, (SPAN + 1) * ROWS, ROWS), BF16),
+                pltpu.VMEM((NX, 8, ROWS), F32),
+                pltpu.VMEM((8, ROWS), F32),
+            ),
             in_specs=[hbm] * 12,
-            out_specs=(pl.BlockSpec(memory_space=pltpu.VMEM),) * 2,
+            out_specs=(pl.BlockSpec(memory_space=pltpu.VMEM),) * 5,
             scratch_shapes=[
                 *(pltpu.VMEM((rows, lanes), BF16),) * 3,
                 pltpu.VMEM((rows, lanes), F32),
@@ -402,12 +408,8 @@
                 pltpu.VMEM(((SPAN + 1) * ROWS, lanes), BF16),
                 pltpu.VMEM(square, BF16),
                 pltpu.VMEM(square, BF16),
-                pltpu.VMEM((SPAN + 1, NX, HEAD, ROWS), BF16),
-                pltpu.VMEM((NX, (SPAN + 1) * ROWS, ROWS), BF16),
-                pltpu.VMEM((NX, 8, ROWS), F32),
                 pltpu.VMEM((2 * NX, 8, ROWS), F32),
                 pltpu.VMEM((n_mp, 8, ROWS), F32),
-                pltpu.VMEM((8, ROWS), F32),
                 pltpu.SemaphoreType.DMA((14,)),
                 pltpu.SemaphoreType.DMA((18,)),
                 pltpu.SemaphoreType.DMA((14,)),
@@ -418,13 +420,13 @@
             cost_estimate=pl.CostEstimate(flops=2 * 10**9, bytes_accessed=2 * 10**6, transcendentals=4 * 10**5),
         )(*operands)
         return pl.pallas_call(
-            hand_over,
+            attend,
             out_shape=(jax.ShapeDtypeStruct((rows, lanes), BF16),) * 2,
-            in_specs=[pl.BlockSpec(memory_space=pltpu.VMEM)] * 2,
+            in_specs=[pl.BlockSpec(memory_space=pltpu.VMEM)] * 5,
             out_specs=(hbm,) * 2,
-            scratch_shapes=[pltpu.SemaphoreType.DMA((2,))],
+            scratch_shapes=[pltpu.VMEM((rows, lanes), BF16), pltpu.SemaphoreType.DMA((NX + 1,))],
             compiler_params=pltpu.CompilerParams(vmem_limit_bytes=8 * 2**20),
-        )(mixer, attended)
+        )(*held)
 
     return jax.shard_map(
         local,

time: 42.9 us -> 42.1 us (0.981)
  Pallas kernels: 42.1 us -> 41.4 us
    pallas_call x1, Pallas kernels: 41.4 us -> 40.3 us  [local(): pl.pallas_call(functools.partial(kernel, blocks, n_mp, n_mp * lanes), out...]
where the time goes in v7:
time: 42.1 us; the launch traced here: 42 us
  Pallas kernels  41.4 us (98%)
  between operations  0.64 us (2%)
    pallas_call x1, Pallas kernels, local(): pl.pallas_call(functools.partial(kernel, blocks, n_mp, n_mp * lanes), out...  40.3 us
    pallas_call x1, Pallas kernels, local(): pl.pallas_call(attend, out_shape=(jax.ShapeDtypeStruct((rows, lanes), BF1...  1.08 us

profile of v7, /device:TPU:1, one launch (start us, length us, event | category | flops | bytes accessed | tf_op | source)
XLA Modules:
  0.0 42.0 jit_solution(14888228097764304420)
XLA Ops:
  0.6 40.3 %shard_map.131 = (bf16[128,512]{1,0:T(8,128)(2,1)S(1)}, bf16[5,4,128,128]{3,2,1,0:T(8,128)(2,1)S(1)}, bf16[4,640,128]{2,1,0:T(8,128)(2,1)S(1)}, f32[4,8,128]{2,1,0:T(8,128)S(1)}, f32[8,128]{1,0:T(8,128)S(1)}) custom-call(bf16[128,512]{1,0:T(8,128)(2,1)} %gate_hbm.1, bf16[128,512]{1,0:T(8,128)(2,1)} %value_hbm.1, bf16[128,512]{1,0:T(8,128)(2,1)} %out_gate_hbm.1, ...), custom_call_target="tpu_custom_call" | custom-call | flops 2000000000 | bytes 2000000 | tf_op jit(solution)/shard_map/pallas_call | solution.py:385
  40.9 1.1 %shard_map.132 = (bf16[128,512]{1,0:T(8,128)(2,1)}, bf16[128,512]{1,0:T(8,128)(2,1)}) custom-call(bf16[128,512]{1,0:T(8,128)(2,1)S(1)} %get-tuple-element.7.mixer_from, bf16[5,4,128,128]{3,2,1,0:T(8,128)(2,1)S(1)} %get-tuple-element.8.value_all, bf16[4,640,128]{2,1,0:T(8,128)(2,1)S(1)} %get-tuple-element.9.probs, f32[4,8,128]{2,1,0:T(8,128)S(1)} %get-tuple-element.10.denoms, ...), custom_call_target="tpu_custom_call" | custom-call | tf_op jit(solution)/shard_map/pallas_call | solution.py:422

commit v8 on v7

--- a/solution.py
+++ b/solution.py
@@ -188,7 +188,7 @@
         return value[:, c * ROWS:(c + 1) * ROWS]
 
     def forward(recv):
-        work[...] = recv[...].astype(F32)
+        work[all_rows] = recv[...].astype(F32)
         panel = jnp.concatenate([work[pl.ds(c, blocks, stride=width), :] for c in range(width)], 1).astype(BF16)
         panel = jnp.concatenate([panel, panel], 0)
         bins = jnp.dot(first_ref[...], panel, preferred_element_type=F32)
@@ -199,7 +199,7 @@
             rows.append(jnp.concatenate([a * twist_real - b * twist_imag, a * twist_imag + b * twist_real], 1))
         return times_wide(jnp.concatenate(rows, 0), 0)
 
-    remote_rows = pl.ds(0, (blocks - 1) * width)
+    remote_rows, all_rows = pl.ds(0, (blocks - 1) * width), pl.ds(0, blocks * width)
     received(recv_taps.at[remote_rows], 0)
     spectrum[...] = forward(recv_taps)
     skip_at = x * HEAD + y * width
@@ -221,7 +221,7 @@
     convolved = jnp.dot(last_ref[...], jnp.concatenate([high, high, low], 0), preferred_element_type=F32)
     for c in range(width):
         work[pl.ds(c, blocks, stride=width), :] = lane_tile(convolved, c)
-    back_send[...] = work[...].astype(BF16).reshape(blocks, width, ROWS)
+    back_send[...] = work[all_rows].astype(BF16).reshape(blocks, width, ROWS)
 
     def send_back(k, carry):
         py = lax.rem(y + far_first(k, n_y), n_y)
@@ -330,9 +330,6 @@
         received(value_all.at[:, h], 8 + h)
         mixer_out[:, pl.ds(h * HEAD, HEAD)] = value_all[SPAN, h].astype(F32).T.astype(BF16)
 
-    received(power_mp.at[pl.ds(0, n_mp - 1)], 12)
-    scales[...] = lax.rsqrt(jnp.sum(power_mp[...], 0) * (1.0 / model) + 1e-06)
-
     sent(recv_taps.at[remote_rows], 0)
     sent(recv_signal.at[remote_rows], 1)
     sent(gate_head.at[pl.ds(0, NX - 1)], 2)
@@ -351,6 +348,9 @@
             sent(value_row.at[pl.ds(0, px + 1)], 9 + px)
             sent(value_row.at[pl.ds(0, NX - px)], 14 + px)
     sent(power_mp.at[pl.ds(0, n_mp - 1)], 13)
+
+    received(power_mp.at[pl.ds(0, n_mp - 1)], 12)
+    scales[...] = lax.rsqrt(jnp.sum(power_mp[...], 0) * (1.0 / model) + 1e-06)
 
 
 def attend(mixer_from, value_all, probs, denoms, scales, mixer_to, attended_to, attended, sems):
@@ -400,7 +400,7 @@
                 pltpu.SMEM((lanes,), F32),
                 *(pltpu.VMEM(c.shape, c.dtype) for c in constants),
                 *(pltpu.VMEM((lanes, ROWS), BF16),) * 5,
-                pltpu.VMEM((lanes, ROWS), F32),
+                pltpu.VMEM((lanes + width, ROWS), F32),
                 pltpu.VMEM((lanes, 2 * ROWS), F32),
                 pltpu.VMEM(square, BF16),
                 pltpu.VMEM((blocks, width, ROWS), BF16),

time: 42.1 us -> 42.1 us (level)
  no operation moved by 1% of the time
where the time goes in v8:
time: 42.1 us; the launch traced here: 42 us
  Pallas kernels  41.3 us (98%)
  between operations  0.64 us (2%)
    pallas_call x1, Pallas kernels, local(): pl.pallas_call(functools.partial(kernel, blocks, n_mp, n_mp * lanes), out...  40.3 us
    pallas_call x1, Pallas kernels, local(): pl.pallas_call(attend, out_shape=(jax.ShapeDtypeStruct((rows, lanes), BF1...  1.08 us

profile of v8, /device:TPU:1, one launch (start us, length us, event | category | flops | bytes accessed | tf_op | source)
XLA Modules:
  0.0 42.0 jit_solution(14218725528762352612)
XLA Ops:
  0.6 40.3 %shard_map.131 = (bf16[128,512]{1,0:T(8,128)(2,1)S(1)}, bf16[5,4,128,128]{3,2,1,0:T(8,128)(2,1)S(1)}, bf16[4,640,128]{2,1,0:T(8,128)(2,1)S(1)}, f32[4,8,128]{2,1,0:T(8,128)S(1)}, f32[8,128]{1,0:T(8,128)S(1)}) custom-call(bf16[128,512]{1,0:T(8,128)(2,1)} %gate_hbm.1, bf16[128,512]{1,0:T(8,128)(2,1)} %value_hbm.1, bf16[128,512]{1,0:T(8,128)(2,1)} %out_gate_hbm.1, ...), custom_call_target="tpu_custom_call" | custom-call | flops 2000000000 | bytes 2000000 | tf_op jit(solution)/shard_map/pallas_call | solution.py:385
  40.9 1.1 %shard_map.132 = (bf16[128,512]{1,0:T(8,128)(2,1)}, bf16[128,512]{1,0:T(8,128)(2,1)}) custom-call(bf16[128,512]{1,0:T(8,128)(2,1)S(1)} %get-tuple-element.7.mixer_from, bf16[5,4,128,128]{3,2,1,0:T(8,128)(2,1)S(1)} %get-tuple-element.8.value_all, bf16[4,640,128]{2,1,0:T(8,128)(2,1)S(1)} %get-tuple-element.9.probs, f32[4,8,128]{2,1,0:T(8,128)S(1)} %get-tuple-element.10.denoms, ...), custom_call_target="tpu_custom_call" | custom-call | tf_op jit(solution)/shard_map/pallas_call | solution.py:422

commit v9 on v8

--- a/solution.py
+++ b/solution.py
@@ -262,7 +262,9 @@
 
     @pl.when(y < n_y - 1)
     def _():
-        send(value_row, value_old, 13, {"ctx": next_row}, 8)
+        for half in (1, 0):
+            part = pl.ds(2 * half, 2)
+            send(value_row.at[part], value_old.at[part], 13 + half, {"ctx": next_row}, 8 + 10 * half)
 
     for px in range(NX):
         src, dst = value_row.at[pl.ds(0, px + 1)], value_all.at[pl.ds(SPAN - px, px + 1), x]
@@ -295,20 +297,23 @@
 
     lax.fori_loop(0, n_mp - 1, share_power, 0)
 
-    @pl.when(y > 0)
-    def _():
-        received(value_old, 13)
-
-    for px in range(NX):
-        src, dst = value_old.at[pl.ds(px, NX - px)], value_all.at[pl.ds(0, NX - px), x]
-
-        @pl.when(x != px)
-        def _():
-            send(src, dst, 8 + x, {"ctx": y * NX + px}, 14 + px)
-
-        @pl.when(x == px)
-        def _():
-            pltpu.make_async_copy(src, dst, recv_sems.at[8 + x]).start()
+    for half in (1, 0):
+        @pl.when(y > 0)
+        def _():
+            received(value_old.at[pl.ds(2 * half, 2)], 13 + half)
+
+        for px in range(2 * half + 2):
+            first = max(px, 2 * half)
+            count = 2 * half + 2 - first
+            src, dst = value_old.at[pl.ds(first, count)], value_all.at[pl.ds(first - px, count), x]
+
+            @pl.when(x != px)
+            def _():
+                send(src, dst, 8 + x, {"ctx": y * NX + px}, 14 + px)
+
+            @pl.when(x == px)
+            def _():
+                pltpu.make_async_copy(src, dst, recv_sems.at[8 + x]).start()
 
     received(key_all.at[pl.ds(0, (NX - 1) * ROWS)], 4)
     reach = (SPAN + 1) * ROWS
@@ -337,7 +342,8 @@
     def _():
         sent(oldest_keys, 3)
         sent(power_x.at[pl.ds(0, NX)], 7)
-        sent(value_row, 8)
+        sent(value_row.at[pl.ds(0, 2)], 8)
+        sent(value_row.at[pl.ds(2, 2)], 18)
 
     sent(key_all.at[pl.ds(0, (NX - 1) * ROWS)], 4)
     sent(back_send.at[pl.ds(0, (n_y - 1) * NX)], 5)
@@ -355,8 +361,7 @@
 
 def attend(mixer_from, value_all, probs, denoms, scales, mixer_to, attended_to, attended, sems):
     x = lax.rem(lax.axis_index("ctx"), NX)
-    copies = [pltpu.make_async_copy(mixer_from, mixer_to, sems.at[NX])]
-    copies[0].start()
+    copies = []
     for h in range(NX):
         values = [
             (value_all[j, h].astype(F32) * scales[pl.ds(x + j, 1), :]).astype(BF16) for j in range(SPAN + 1)
@@ -366,6 +371,9 @@
         attended[:, lanes] = (summed / denoms[h][0:1]).T.astype(BF16)
         copies.append(pltpu.make_async_copy(attended.at[:, lanes], attended_to.at[:, lanes], sems.at[h]))
         copies[-1].start()
+        if h == 0:
+            copies.append(pltpu.make_async_copy(mixer_from, mixer_to, sems.at[NX]))
+            copies[-1].start()
     for copy in copies:
         copy.wait()
 
@@ -411,8 +419,8 @@
                 pltpu.VMEM((2 * NX, 8, ROWS), F32),
                 pltpu.VMEM((n_mp, 8, ROWS), F32),
                 pltpu.SemaphoreType.DMA((14,)),
-                pltpu.SemaphoreType.DMA((18,)),
-                pltpu.SemaphoreType.DMA((14,)),
+                pltpu.SemaphoreType.DMA((19,)),
+                pltpu.SemaphoreType.DMA((15,)),
             ],
             compiler_params=pltpu.CompilerParams(
                 collective_id=0, has_side_effects=True, vmem_limit_bytes=32 * 2**20

time: 42.1 us -> 42.1 us (level)
  no operation moved by 1% of the time
where the time goes in v9:
time: 42.1 us; the launch traced here: 42 us
  Pallas kernels  41.4 us (98%)
  between operations  0.64 us (2%)
    pallas_call x1, Pallas kernels, local(): pl.pallas_call(functools.partial(kernel, blocks, n_mp, n_mp * lanes), out...  40.3 us
    pallas_call x1, Pallas kernels, local(): pl.pallas_call(attend, out_shape=(jax.ShapeDtypeStruct((rows, lanes), BF1...  1.08 us

profile of v9, /device:TPU:1, one launch (start us, length us, event | category | flops | bytes accessed | tf_op | source)
XLA Modules:
  0.0 42.0 jit_solution(12714755706466224522)
XLA Ops:
  0.6 40.3 %shard_map.131 = (bf16[128,512]{1,0:T(8,128)(2,1)S(1)}, bf16[5,4,128,128]{3,2,1,0:T(8,128)(2,1)S(1)}, bf16[4,640,128]{2,1,0:T(8,128)(2,1)S(1)}, f32[4,8,128]{2,1,0:T(8,128)S(1)}, f32[8,128]{1,0:T(8,128)S(1)}) custom-call(bf16[128,512]{1,0:T(8,128)(2,1)} %gate_hbm.1, bf16[128,512]{1,0:T(8,128)(2,1)} %value_hbm.1, bf16[128,512]{1,0:T(8,128)(2,1)} %out_gate_hbm.1, ...), custom_call_target="tpu_custom_call" | custom-call | flops 2000000000 | bytes 2000000 | tf_op jit(solution)/shard_map/pallas_call | solution.py:393
  40.9 1.1 %shard_map.132 = (bf16[128,512]{1,0:T(8,128)(2,1)}, bf16[128,512]{1,0:T(8,128)(2,1)}) custom-call(bf16[128,512]{1,0:T(8,128)(2,1)S(1)} %get-tuple-element.7.mixer_from, bf16[5,4,128,128]{3,2,1,0:T(8,128)(2,1)S(1)} %get-tuple-element.8.value_all, bf16[4,640,128]{2,1,0:T(8,128)(2,1)S(1)} %get-tuple-element.9.probs, f32[4,8,128]{2,1,0:T(8,128)S(1)} %get-tuple-element.10.denoms, ...), custom_call_target="tpu_custom_call" | custom-call | tf_op jit(solution)/shard_map/pallas_call | solution.py:430

commit v10 on v8

--- a/solution.py
+++ b/solution.py
@@ -323,7 +323,7 @@
         ) * (1.0 / math.sqrt(HEAD))
         scores = jnp.where(allowed, scores, -1e30)
         weights = jnp.exp(scores - jnp.max(scores, 0, keepdims=True))
-        denoms[h] = jnp.broadcast_to(jnp.sum(weights, 0, keepdims=True), (8, ROWS))
+        denoms[h] = jnp.broadcast_to(1.0 / jnp.sum(weights, 0, keepdims=True), (8, ROWS))
         probs[h] = weights.astype(BF16)
 
     for h in range(NX):
@@ -363,7 +363,7 @@
         ]
         summed = jnp.dot(jnp.concatenate(values, 1), probs[h], preferred_element_type=F32)
         lanes = pl.ds(h * HEAD, HEAD)
-        attended[:, lanes] = (summed / denoms[h][0:1]).T.astype(BF16)
+        attended[:, lanes] = (summed * denoms[h][0:1]).T.astype(BF16)
         copies.append(pltpu.make_async_copy(attended.at[:, lanes], attended_to.at[:, lanes], sems.at[h]))
         copies[-1].start()
     for copy in copies:

time: 42.1 us -> 42.1 us (level)
  no operation moved by 1% of the time
where the time goes in v10:
time: 42.1 us; the launch traced here: 42 us
  Pallas kernels  41.3 us (98%)
  between operations  0.64 us (2%)
    pallas_call x1, Pallas kernels, local(): pl.pallas_call(functools.partial(kernel, blocks, n_mp, n_mp * lanes), out...  40.3 us
    pallas_call x1, Pallas kernels, local(): pl.pallas_call(attend, out_shape=(jax.ShapeDtypeStruct((rows, lanes), BF1...  1.08 us

profile of v10, /device:TPU:1, one launch (start us, length us, event | category | flops | bytes accessed | tf_op | source)
XLA Modules:
  0.0 42.0 jit_solution(1000012815509283829)
XLA Ops:
  0.6 40.3 %shard_map.131 = (bf16[128,512]{1,0:T(8,128)(2,1)S(1)}, bf16[5,4,128,128]{3,2,1,0:T(8,128)(2,1)S(1)}, bf16[4,640,128]{2,1,0:T(8,128)(2,1)S(1)}, f32[4,8,128]{2,1,0:T(8,128)S(1)}, f32[8,128]{1,0:T(8,128)S(1)}) custom-call(bf16[128,512]{1,0:T(8,128)(2,1)} %gate_hbm.1, bf16[128,512]{1,0:T(8,128)(2,1)} %value_hbm.1, bf16[128,512]{1,0:T(8,128)(2,1)} %out_gate_hbm.1, ...), custom_call_target="tpu_custom_call" | custom-call | flops 2000000000 | bytes 2000000 | tf_op jit(solution)/shard_map/pallas_call | solution.py:385
  40.9 1.1 %shard_map.132 = (bf16[128,512]{1,0:T(8,128)(2,1)}, bf16[128,512]{1,0:T(8,128)(2,1)}) custom-call(bf16[128,512]{1,0:T(8,128)(2,1)S(1)} %get-tuple-element.7.mixer_from, bf16[5,4,128,128]{3,2,1,0:T(8,128)(2,1)S(1)} %get-tuple-element.8.value_all, bf16[4,640,128]{2,1,0:T(8,128)(2,1)S(1)} %get-tuple-element.9.probs, f32[4,8,128]{2,1,0:T(8,128)S(1)} %get-tuple-element.10.denoms, ...), custom_call_target="tpu_custom_call" | custom-call | tf_op jit(solution)/shard_map/pallas_call | solution.py:422
